TPU v7x, 128 devices: a whole 4x4x4 slice. The times are simulated.
128 devices in a mesh: ctx: 64 (over x_hi, y, z, core), head: 2 (over x_lo).
Axes of the slice: x: 4 (x_hi: 2, x_lo: 2; x = x_hi * 2 + x_lo), y: 4, z: 4, core: 2. Of those that a mesh axis runs over, the one named last changes fastest.
Arguments:
- hidden_in: bfloat16 [16384, 768], P(('ctx', 'head')), may hold values from -6 to 6
- ln1_gain: bfloat16 [768], P('ctx'), may hold values from 0.099609375 to 1.8984375
- ln1_shift: bfloat16 [768], P('ctx'), may hold values from -1.5 to 1.5
- w_qkv: bfloat16 [768, 2304], P('ctx'), may hold values from -0.3125 to 0.3125
- qv_bias: bfloat16 [1536], P('ctx'), may hold values from -1.5 to 1.5
- w_out: bfloat16 [768, 768], P('ctx'), may hold values from -1.5 to 1.5
- out_bias: bfloat16 [768], P('ctx'), may hold values from -1.5 to 1.5
- ln2_gain: bfloat16 [768], P('ctx'), may hold values from 0.099609375 to 1.8984375
- ln2_shift: bfloat16 [768], P('ctx'), may hold values from -1.5 to 1.5
- w_fc: bfloat16 [768, 3072], P('ctx'), may hold values from -0.21875 to 0.21875
- fc_bias: bfloat16 [3072], P('ctx'), may hold values from -2.5 to 2.5
- w_proj: bfloat16 [3072, 768], P('ctx'), may hold values from -0.21875 to 0.21875
- proj_bias: bfloat16 [768], P('ctx'), may hold values from -1.5 to 1.5
- out_grad: bfloat16 [16384, 768], P(('ctx', 'head')), may hold values from -6 to 6
Outputs:
- hidden_out: bfloat16 [16384, 768], P(('ctx', 'head'))
- input_grad: float32 [16384, 768], P(('ctx', 'head'))
- ln1_gain_grad: float32 [768], P('ctx')
- ln1_shift_grad: float32 [768], P('ctx')
- w_qkv_grad: float32 [768, 2304], P('ctx')
- qv_bias_grad: float32 [1536], P('ctx')
- w_out_grad: float32 [768, 768], P('ctx')
- out_bias_grad: float32 [768], P('ctx')
- ln2_gain_grad: float32 [768], P('ctx')
- ln2_shift_grad: float32 [768], P('ctx')
- w_fc_grad: float32 [768, 3072], P('ctx')
- fc_bias_grad: float32 [3072], P('ctx')
- w_proj_grad: float32 [3072, 768], P('ctx')
- proj_bias_grad: float32 [768], P('ctx')
All inputs are finite; a program needn't handle non-finite values.
Results may differ from a plain program's by a relative error of at most 0.018.
Values may be sent and summed in bfloat16 or wider, within the bound.
A program may use at most 256 MiB of HBM per device.

v0:
```python
import jax
import jax.numpy as jnp
from jax import lax
from jax.sharding import PartitionSpec as P

D = 768
HEAD_DIM = 64
KEY_BLOCK = 512


EPS = 1e-05
NEG = -1e30


def side_by_side(arrays, axis, dim, along):
    columns = [a.reshape(*a.shape[:along], -1) for a in arrays]
    both = jnp.concatenate(columns, axis=along)
    filled, at, gathered = (lax.all_gather(both, axis, axis=dim, tiled=True), 0, [])
    for a, column in zip(arrays, columns):
        section = filled[..., at : at + column.shape[along]]
        gathered.append(section.reshape(*section.shape[:along], *a.shape[along:]))
        at += column.shape[along]
    return tuple(gathered)


def in_one_piece(arrays, axis, dim, along):
    widths = [a.shape[along] for a in arrays]
    both = jnp.concatenate(arrays, axis=along)
    filled = lax.all_gather(both, axis, axis=dim, tiled=True)
    return tuple(jnp.split(filled, [sum(widths[:k]) for k in range(1, len(widths))], axis=along))


def cut_along(value, dim, devices):
    dims = value.shape
    tiles = value.reshape(*dims[:dim], devices, dims[dim] // devices, *dims[dim + 1 :])
    return jnp.moveaxis(tiles, dim, 0)


def sum_together(arrays, axis, dims):
    devices = lax.axis_size(axis)
    tiles = [cut_along(a, dim, devices) for a, dim in zip(arrays, dims)]
    lines = jnp.concatenate([b.reshape(devices, -1) for b in tiles], axis=1)
    span = max(16, -(-lines.shape[1] // 1024) * 8)
    lines = jnp.pad(lines, ((0, 0), (0, span * 128 - lines.shape[1]))).reshape(-1, 128)
    line, at, gathered = (lax.psum_scatter(lines, axis, tiled=True).reshape(-1), 0, [])
    for b in tiles:
        part = b[0]
        gathered.append(line[at : at + part.size].reshape(part.shape))
        at += part.size
    return tuple(gathered)


def sent_to_all(value, axis):
    devices = lax.axis_size(axis)
    return lax.all_to_all(
        jnp.broadcast_to(value[None], (devices, *value.shape)), axis, 0, 0, tiled=True
    )


def of_everyone(value, axis):
    everything = sent_to_all(value, axis)
    return jnp.sum(everything.astype(jnp.float32), axis=0)


def layer_norm(values, gain, shift):
    mean = jnp.mean(values, axis=-1, keepdims=True)
    centred = values - mean
    spread = jnp.mean(centred * centred, axis=-1, keepdims=True)
    return centred * lax.rsqrt(spread + EPS) * gain + shift


def gelu_tanh(values):
    return jax.nn.gelu(values, approximate=True)


def matmul(left, right):
    return jnp.dot(left, right, preferred_element_type=jnp.float32)


def trans_left(left, right):
    return lax.dot_general(
        left, right, (((0,), (0,)), ((), ())), preferred_element_type=jnp.float32
    )


def trans_right(left, right):
    return lax.dot_general(
        left, right, (((1,), (1,)), ((), ())), preferred_element_type=jnp.float32
    )


def masked_scores(queries, keys, query_start, key_start):
    scores = jnp.einsum(
        "qhd,khd->hqk", queries, keys, preferred_element_type=jnp.float32
    ) * HEAD_DIM ** (-0.5)
    query_pos = query_start + jnp.arange(queries.shape[0], dtype=jnp.int32)
    key_pos = key_start + jnp.arange(keys.shape[0], dtype=jnp.int32)
    allowed = (key_pos[None, :] <= query_pos[:, None])[None]
    return (jnp.where(allowed, scores, NEG), allowed)


def score_grads(
    query_blk, grad_blk, key_blk, value_blk, query_start, key_start, lse_blk, delta_blk
):
    scores, allowed = masked_scores(query_blk, key_blk, query_start, key_start)
    weights = jnp.where(allowed, jnp.exp(scores - lse_blk[..., None]), 0.0)
    grad_weights = jnp.einsum(
        "qhd,khd->hqk", grad_blk, value_blk, preferred_element_type=jnp.float32
    )
    grad_scores = (weights * (grad_weights - delta_blk[..., None])).astype(jnp.bfloat16)
    return (weights.astype(jnp.bfloat16), grad_scores)


def on_device(
    hidden_in,
    ln1_gain,
    ln1_shift,
    w_qkv,
    qv_bias,
    w_out,
    out_bias,
    ln2_gain,
    ln2_shift,
    w_fc,
    fc_bias,
    w_proj,
    proj_bias,
    out_grad,
):
    (
        ln1_gain,
        ln1_shift,
        w_qkv,
        qv_bias,
        w_out,
        out_bias,
        ln2_gain,
        ln2_shift,
        w_fc,
        fc_bias,
        w_proj,
        proj_bias,
    ) = (
        lax.all_gather(ln1_gain, "ctx", axis=0, tiled=True),
        *side_by_side((ln1_shift, w_qkv), "ctx", 0, 1),
        lax.all_gather(qv_bias, "ctx", axis=0, tiled=True),
        *side_by_side((w_out, out_bias, ln2_gain, ln2_shift, w_fc), "ctx", 0, 1),
        *side_by_side((fc_bias, w_proj), "ctx", 0, 1),
        lax.all_gather(proj_bias, "ctx", axis=0, tiled=True),
    )
    gain_one = ln1_gain.astype(jnp.float32)
    shift_one = ln1_shift.astype(jnp.float32)
    gain_two = ln2_gain.astype(jnp.float32)
    shift_two = ln2_shift.astype(jnp.float32)
    bias_qv = qv_bias.astype(jnp.float32)
    scale = HEAD_DIM ** (-0.5)
    resid = hidden_in.astype(jnp.float32)
    low_one = layer_norm(resid, gain_one, shift_one).astype(jnp.bfloat16)
    projected = matmul(low_one, w_qkv)
    queries = (projected[:, :D] + bias_qv[:D]).astype(jnp.bfloat16)
    keys = projected[:, D : 2 * D].astype(jnp.bfloat16)
    values = (projected[:, 2 * D :] + bias_qv[D:]).astype(jnp.bfloat16)
    query_heads, key_heads, value_heads = (
        lax.all_to_all(queries, "head", split_axis=1, concat_axis=0, tiled=True),
        lax.all_to_all(keys, "head", split_axis=1, concat_axis=0, tiled=True),
        lax.all_to_all(values, "head", split_axis=1, concat_axis=0, tiled=True),
    )
    rows = query_heads.shape[0]
    local_heads = query_heads.shape[1] // HEAD_DIM
    query_three = query_heads.reshape(rows, local_heads, HEAD_DIM)
    key_all, value_all = in_one_piece((key_heads, value_heads), "ctx", 0, 1)
    seq = key_all.shape[0]
    key_three = key_all.reshape(seq, local_heads, HEAD_DIM)
    value_three = value_all.reshape(seq, local_heads, HEAD_DIM)
    query_start = lax.axis_index("ctx") * rows
    block_count = (query_start + rows + KEY_BLOCK - 1) // KEY_BLOCK

    def stat_step(block, carry):
        top, total = carry
        start = block * KEY_BLOCK
        key_blk = lax.dynamic_slice_in_dim(key_three, start, KEY_BLOCK, 0)
        scores, allowed = masked_scores(query_three, key_blk, query_start, start)
        new_top = jnp.maximum(top, jnp.max(scores, axis=-1))
        total = total * jnp.exp(top - new_top) + jnp.sum(
            jnp.exp(scores - new_top[..., None]), axis=-1
        )
        return (new_top, total)

    top, total = lax.fori_loop(
        0,
        block_count,
        stat_step,
        (
            jnp.full((local_heads, rows), NEG, jnp.float32),
            jnp.zeros((local_heads, rows), jnp.float32),
        ),
    )
    lse = top + jnp.log(total)

    def out_step(block, accum):
        start = block * KEY_BLOCK
        key_blk = lax.dynamic_slice_in_dim(key_three, start, KEY_BLOCK, 0)
        value_blk = lax.dynamic_slice_in_dim(value_three, start, KEY_BLOCK, 0)
        scores, allowed = masked_scores(query_three, key_blk, query_start, start)
        weights = jnp.where(allowed, jnp.exp(scores - lse[..., None]), 0.0).astype(jnp.bfloat16)
        return accum + jnp.einsum(
            "hqk,khd->qhd", weights, value_blk, preferred_element_type=jnp.float32
        )

    attended = lax.fori_loop(
        0, block_count, out_step, jnp.zeros((rows, local_heads, HEAD_DIM), jnp.float32)
    )
    attended_tok = lax.all_to_all(
        attended.reshape(rows, -1).astype(jnp.bfloat16),
        "head",
        split_axis=0,
        concat_axis=1,
        tiled=True,
    )
    mid = resid + matmul(attended_tok, w_out) + out_bias.astype(jnp.float32)
    low_two = layer_norm(mid, gain_two, shift_two).astype(jnp.bfloat16)
    pre_fc = matmul(low_two, w_fc) + fc_bias.astype(jnp.float32)
    activ = gelu_tanh(pre_fc).astype(jnp.bfloat16)
    output = mid + matmul(activ, w_proj) + proj_bias.astype(jnp.float32)
    hidden_out = output.astype(jnp.bfloat16)
    grad_output = out_grad.astype(jnp.float32)
    grad_wproj = trans_left(activ, out_grad)
    grad_bproj = jnp.sum(grad_output, axis=0)
    grad_activ = trans_right(out_grad, w_proj)
    gelu_pull = jax.vjp(gelu_tanh, pre_fc)[1]
    grad_pre = gelu_pull(grad_activ)[0].astype(jnp.bfloat16)
    grad_wfc = trans_left(low_two, grad_pre)
    grad_bfc = jnp.sum(grad_pre.astype(jnp.float32), axis=0)
    grad_norm2 = trans_right(grad_pre, w_fc)
    norm2_pull = jax.vjp(layer_norm, mid, gain_two, shift_two)[1]
    grad_mid_ln, grad_gain2, grad_shift2 = norm2_pull(grad_norm2)
    grad_mid = grad_output + grad_mid_ln
    grad_attn = grad_mid.astype(jnp.bfloat16)
    grad_wout = trans_left(attended_tok, grad_attn)
    grad_bout = jnp.sum(grad_attn.astype(jnp.float32), axis=0)
    grad_attended = trans_right(grad_attn, w_out).astype(jnp.bfloat16)
    grad_heads = lax.all_to_all(grad_attended, "head", split_axis=1, concat_axis=0, tiled=True)
    grad_three = grad_heads.reshape(rows, local_heads, HEAD_DIM)
    delta = jnp.einsum("qhd,qhd->hq", grad_three.astype(jnp.float32), attended)

    def query_step(block, grad_query):
        start = block * KEY_BLOCK
        key_blk = lax.dynamic_slice_in_dim(key_three, start, KEY_BLOCK, 0)
        value_blk = lax.dynamic_slice_in_dim(value_three, start, KEY_BLOCK, 0)
        weights, grad_scores = score_grads(
            query_three, grad_three, key_blk, value_blk, query_start, start, lse, delta
        )
        return grad_query + scale * jnp.einsum(
            "hqk,khd->qhd", grad_scores, key_blk, preferred_element_type=jnp.float32
        )

    grad_query = lax.fori_loop(
        0, block_count, query_step, jnp.zeros((rows, local_heads, HEAD_DIM), jnp.float32)
    )
    query_all, grad_all = in_one_piece((query_heads, grad_heads), "ctx", 0, 1)
    lse_all, delta_all = in_one_piece((lse.T, delta.T), "ctx", 0, 1)
    query_all = query_all.reshape(seq, local_heads, HEAD_DIM)
    grad_all = grad_all.reshape(seq, local_heads, HEAD_DIM)
    key_own = key_heads.reshape(rows, local_heads, HEAD_DIM)
    value_own = value_heads.reshape(rows, local_heads, HEAD_DIM)

    def key_step(block, carry):
        grad_keys, grad_values = carry
        start = block * KEY_BLOCK
        query_blk = lax.dynamic_slice_in_dim(query_all, start, KEY_BLOCK, 0)
        grad_blk = lax.dynamic_slice_in_dim(grad_all, start, KEY_BLOCK, 0)
        lse_blk = lax.dynamic_slice_in_dim(lse_all, start, KEY_BLOCK, 0).T
        delta_blk = lax.dynamic_slice_in_dim(delta_all, start, KEY_BLOCK, 0).T
        weights, grad_scores = score_grads(
            query_blk, grad_blk, key_own, value_own, start, query_start, lse_blk, delta_blk
        )
        grad_keys = grad_keys + scale * jnp.einsum(
            "hqk,qhd->khd", grad_scores, query_blk, preferred_element_type=jnp.float32
        )
        grad_values = grad_values + jnp.einsum(
            "hqk,qhd->khd", weights, grad_blk, preferred_element_type=jnp.float32
        )
        return (grad_keys, grad_values)

    empty_own = jnp.zeros((rows, local_heads, HEAD_DIM), jnp.float32)
    grad_keys, grad_values = lax.fori_loop(
        query_start // KEY_BLOCK, seq // KEY_BLOCK, key_step, (empty_own, empty_own)
    )
    grad_keys = grad_keys.reshape(rows, -1)
    grad_values = grad_values.reshape(rows, -1)
    grad_q_tok, grad_k_tok, grad_v_tok = (
        lax.all_to_all(
            grad_query.reshape(rows, -1).astype(jnp.bfloat16),
            "head",
            split_axis=0,
            concat_axis=1,
            tiled=True,
        ),
        lax.all_to_all(
            grad_keys.astype(jnp.bfloat16), "head", split_axis=0, concat_axis=1, tiled=True
        ),
        lax.all_to_all(
            grad_values.astype(jnp.bfloat16), "head", split_axis=0, concat_axis=1, tiled=True
        ),
    )
    grad_qkv = jnp.concatenate([grad_q_tok, grad_k_tok, grad_v_tok], axis=1)
    grad_wqkv = trans_left(low_one, grad_qkv)
    grad_bqv = jnp.concatenate(
        [
            jnp.sum(grad_q_tok.astype(jnp.float32), axis=0),
            jnp.sum(grad_v_tok.astype(jnp.float32), axis=0),
        ]
    )
    grad_norm1 = trans_right(grad_qkv, w_qkv)
    norm1_pull = jax.vjp(layer_norm, resid, gain_one, shift_one)[1]
    grad_in_ln, grad_gain1, grad_shift1 = norm1_pull(grad_norm1)
    input_grad = grad_mid + grad_in_ln
    summed = sum_together(
        (
            grad_gain1,
            grad_shift1,
            grad_wqkv,
            grad_bqv,
            grad_wout,
            grad_bout,
            grad_gain2,
            grad_shift2,
            grad_wfc,
            grad_bfc,
            grad_wproj,
            grad_bproj,
        ),
        "ctx",
        (0, 0, 0, 0, 0, 0, 0, 0, 0, 0, 0, 0),
    )
    totals = (
        of_everyone(summed[0].astype(jnp.bfloat16), "head").astype(jnp.float32),
        of_everyone(summed[1].astype(jnp.bfloat16), "head").astype(jnp.float32),
        of_everyone(summed[2].astype(jnp.bfloat16), "head").astype(jnp.float32),
        of_everyone(summed[3].astype(jnp.bfloat16), "head").astype(jnp.float32),
        of_everyone(summed[4].astype(jnp.bfloat16), "head").astype(jnp.float32),
        of_everyone(summed[5].astype(jnp.bfloat16), "head").astype(jnp.float32),
        of_everyone(summed[6].astype(jnp.bfloat16), "head").astype(jnp.float32),
        of_everyone(summed[7].astype(jnp.bfloat16), "head").astype(jnp.float32),
        of_everyone(summed[8].astype(jnp.bfloat16), "head").astype(jnp.float32),
        of_everyone(summed[9].astype(jnp.bfloat16), "head").astype(jnp.float32),
        of_everyone(summed[10].astype(jnp.bfloat16), "head").astype(jnp.float32),
        of_everyone(summed[11].astype(jnp.bfloat16), "head").astype(jnp.float32),
    )
    return (
        hidden_out,
        input_grad,
        totals[0],
        totals[1],
        totals[2],
        totals[3],
        totals[4],
        totals[5],
        totals[6],
        totals[7],
        totals[8],
        totals[9],
        totals[10],
        totals[11],
    )


def solution(mesh):
    in_specs = (
        P(("ctx", "head"), None),
        P("ctx"),
        P("ctx"),
        P("ctx", None),
        P("ctx"),
        P("ctx", None),
        P("ctx"),
        P("ctx"),
        P("ctx"),
        P("ctx", None),
        P("ctx"),
        P("ctx", None),
        P("ctx"),
        P(("ctx", "head"), None),
    )
    out_specs = (
        P(("ctx", "head"), None),
        P(("ctx", "head"), None),
        P("ctx"),
        P("ctx"),
        P("ctx", None),
        P("ctx"),
        P("ctx", None),
        P("ctx"),
        P("ctx"),
        P("ctx"),
        P("ctx", None),
        P("ctx"),
        P("ctx", None),
        P("ctx"),
    )
    return jax.shard_map(
        on_device, mesh=mesh, in_specs=in_specs, out_specs=out_specs, check_vma=False
    )
```

profile of v0, /device:TPU:1, one launch (start us, length us, event | category | flops | bytes accessed | tf_op | source)
XLA Modules:
  0.0 1954.6 jit_solution(18081605787814555831)
XLA Ops:
  21.2 168.5 %all-reduce.5 = (bf16[768]{0:T(1024)(128)(2,1)S(1)}, bf16[1536]{0:T(1024)(128)(2,1)S(1)}, bf16[768]{0:T(1024)(128)(2,1)}) all-reduce(bf16[768]{0:T(1024)(128)(2,1)S(1)} %dynamic-update-slice, bf16[1536]{0:T(1024)(128)(2,1)S(1)} %dynamic-update-slice.1, bf16[768]{0:T(1024)(128)(2,1)S(1)} %dynamic-update-slice.2), channel_id=1, replica_groups=mesh['ctx'=64,'head'=2] {'ctx'}, use_global_device_ids=true, to_apply=%add.1 | all-reduce | flops 3072 | bytes 12288
  192.4 7.4 reshape.517
  208.6 4.0 all-to-all-done.1
  212.6 6.0 all_to_all.208
  223.6 7.1 all-to-all-done.2
  232.5 18.1 all-gather.16.cloned.1.call-done
  250.5 10.6 reshape.519
  261.2 123.8 %all-gather.8.cloned.1.call-done = bf16[16384,768]{1,0:T(8,128)(2,1)} async-done(((bf16[256,768]{1,0:T(8,128)(2,1)}), bf16[16384,768]{1,0:T(8,128)(2,1)}) %all-gather.8.cloned.1.call-update) | async-done | bytes 25165840 | tf_op jit(solution)/shard_map/all_gather | solution.py:29
  385.0 17.2 fusion.136
  402.1 16.7 copy.188
  421.4 16.7 copy.187
  451.4 4.3 fusion.79
  455.7 6.3 convert_reduce_fusion.1
  466.2 6.1 all_to_all.209
  478.2 6.4 fusion.130
  484.6 5.2 fusion.131
  492.5 6.2 while.46
  500.5 4.1 all-to-all-start.5
  504.6 445.2 %all_gather.35 = f32[16384,12]{0,1:T(8,128)S(1)} all-gather(f32[256,12]{0,1:T(8,128)S(1)} %pad_maximum_fusion.7), channel_id=1, replica_groups=mesh['ctx'=64,'head'=2] {'ctx'}, dimensions={0}, use_global_device_ids=true | all-gather | bytes 798720 | tf_op jit(solution)/shard_map/all_gather | solution.py:29
  950.9 17.1 fusion.135
  968.0 15.7 copy.199
  983.7 16.7 copy.201
  1002.0 286.7 %while.47 = (s32[]{:T(128)}, f32[256,6,64]{0,2,1:T(8,128)}, f32[256,6,64]{0,2,1:T(8,128)}, bf16[16384,6,64]{0,2,1:T(8,128)(2,1)}, s32[]{:T(128)}, /*index=5*/bf1...) while((s32[]{:T(128)}, f32[256,6,64]{0,2,1:T(8,128)}, ...), condition=%wide.region_15.16_spmd, body=%wide.region_14.15_spmd.sunk | while | flops 412517120 | bytes 17186104 | solution.py:286
  1007.3 3.6 fusion.201
  1016.3 3.6 fusion.201
  1025.2 3.6 fusion.201
  1034.2 3.6 fusion.201
  1043.2 3.6 fusion.201
  1052.1 3.6 fusion.201
  1061.1 3.6 fusion.201
  1070.0 3.6 fusion.201
  1079.0 3.6 fusion.201
  1088.0 3.6 fusion.201
  1096.9 3.6 fusion.201
  1301.1 11.6 reshape_reshape.14
  1313.5 10.1 reshape_reshape.15
  1332.3 5.2 fusion.122
  1337.5 4.2 fusion.132
  1341.7 7.3 reshape_reshape.12
  1355.9 23.2 %dynamic-update-slice.5 = f32[64,110736]{1,0:T(8,128)} dynamic-update-slice(f32[64,110736]{1,0:T(8,128)} %dynamic-update-slice.4, f32[64,27648]{1,0:T(8,128)} %reshape_reshape.12, s32[]{} %constant.174, s32[]{} %constant.176) | dynamic-update-slice | bytes 14155780
  1380.7 11.5 dynamic-update-slice.7
  1396.9 28.7 %dynamic-update-slice.11 = f32[64,110736]{1,0:T(8,128)} dynamic-update-slice(f32[64,110736]{1,0:T(8,128)} %dynamic-update-slice.10, f32[64,36864]{1,0:T(8,128)} %reshape_reshape.14, s32[]{} %constant.174, s32[]{} %constant.183) | dynamic-update-slice | bytes 18874372
  1427.2 28.3 %dynamic-update-slice.13 = f32[64,110736]{1,0:T(8,128)} dynamic-update-slice(f32[64,110736]{1,0:T(8,128)} %dynamic-update-slice.12, f32[64,36864]{1,0:T(8,128)} %reshape_reshape.15, s32[]{} %constant.174, s32[]{} %constant.185) | dynamic-update-slice | bytes 18874372
  1457.0 20.8 %pad.4 = f32[64,111616]{1,0:T(8,128)} pad(f32[64,110736]{1,0:T(8,128)} %dynamic-update-slice.14, f32[]{:T(128)} %constant.113.clone.1), padding=0_0x0_880 | pad | bytes 56922116 | tf_op jit(solution)/shard_map/jit(_pad)/pad | solution.py:44
  1477.7 21.0 %reshape.499 = f32[55808,128]{1,0:T(8,128)} reshape(f32[64,111616]{1,0:T(8,128)} %pad.4) | data formatting | bytes 57147392 | tf_op jit(solution)/shard_map/reshape | solution.py:44
  1500.2 5.7 fusion.102
  1505.9 360.4 %reduce-scatter.5.cloned.1.call-done = f32[872,128]{1,0:T(8,128)} async-done(((f32[55808,128]{1,0:T(8,128)}), f32[872,128]{1,0:T(8,128)}) %reduce-scatter.5.cloned.1.call-update) | async-done | bytes 446480
  1868.2 5.0 all_to_all.210
  (765 shorter events, 435.2 us)
Async XLA Ops:
  7.2 185.2 %all-gather.14.cloned.1.call-start = ((), (), s32[]{:S(2)}) async-start(), calls=%async_computation.24 | async-start | bytes 5058560 | tf_op jit(solution)/shard_map/all_gather | solution.py:18
  9.6 221.4 %all-gather.10.cloned.1.call-start = ((), (), s32[]{:S(2)}) async-start(), calls=%async_computation.22 | async-start | bytes 5591040 | tf_op jit(solution)/shard_map/all_gather | solution.py:18
  12.1 238.4 %all-gather.16.cloned.1.call-start = ((), (), s32[]{:S(2)}) async-start(), calls=%async_computation.25 | async-start | bytes 8253440 | tf_op jit(solution)/shard_map/all_gather | solution.py:18
  189.7 11.2 copy-start.24
  190.7 10.1 copy-start.34
  205.1 7.5 all-to-all-start.1
  208.5 176.5 %all-gather.8.cloned.1.call-start = ((), (), s32[]{:S(2)}) async-start(), calls=%async_computation.21 | async-start | bytes 25559040 | tf_op jit(solution)/shard_map/all_gather | solution.py:29
  218.6 12.1 copy-start.12
  220.1 10.5 all-to-all-start.2
  230.7 30.5 %copy-start.13 = (bf16[128,2,384]{2,0,1:T(8,128)(2,1)}, bf16[128,2,384]{2,0,1:T(8,128)(2,1)S(1)}, u32[]{:S(2)}) copy-start(bf16[128,2,384]{2,0,1:T(8,128)(2,1)S(1)} %all-to-all-done.2) | copy-start | bytes 589828
  441.5 7.8 all-to-all-start.3
  445.0 505.9 %all-gather.12.cloned.1.call-start = ((), (), s32[]{:S(2)}) async-start(), calls=%async_computation.23 | async-start | bytes 25559040 | tf_op jit(solution)/shard_map/all_gather | solution.py:29
  451.1 27.1 %copy-start.1 = (f32[128,768]{1,0:T(8,128)}, f32[128,768]{1,0:T(8,128)S(1)}, u32[]{:S(2)}) copy-start(f32[128,768]{1,0:T(8,128)S(1)} %get-tuple-element.370) | copy-start | bytes 1179652
  451.1 13.5 copy-start.39
  451.3 13.3 copy-start.40
  451.3 10.7 slice-start
  455.6 29.0 %copy-start.8 = (f32[128,3072]{1,0:T(8,128)}, f32[128,3072]{1,0:T(8,128)S(1)}, u32[]{:S(2)}) copy-start(f32[128,3072]{1,0:T(8,128)S(1)} %fusion.79) | copy-start | bytes 4718596
  464.8 19.7 %copy-start.5 = (f32[128,768]{1,0:T(8,128)}, f32[128,768]{1,0:T(8,128)S(1)}, u32[]{:S(2)}) copy-start(f32[128,768]{1,0:T(8,128)S(1)} %get-tuple-element.344) | copy-start | bytes 1179652
  500.5 789.9 %all-to-all-start.5 = ((bf16[2,128,384]{1,2,0:T(8,128)(2,1)}), bf16[2,128,384]{1,2,0:T(8,128)(2,1)}, u32[]{:S(2)}, u32[]{:S(2)}) async-start(bf16[2,128,384]{1,2,0:T(8,128)(2,1)} %copy.198), calls=%async_computation.5 | async-start | bytes 393216 | tf_op jit(solution)/shard_map/all_to_all | solution.py:292
  983.7 18.3 copy-start.3
  1290.5 33.9 %all-to-all-start.6 = ((bf16[2,128,384]{1,2,0:T(8,128)(2,1)}), bf16[2,128,384]{1,2,0:T(8,128)(2,1)S(1)}, u32[]{:S(2)}, u32[]{:S(2)}) async-start(bf16[2,128,384]{1,2,0:T(8,128)(2,1)} %copy.203), calls=%async_computation.6 | async-start | bytes 393216 | tf_op jit(solution)/shard_map/all_to_all | solution.py:299
  1301.1 11.6 copy-start.36
  1313.4 10.1 copy-start.20
  1313.4 18.8 copy-start.25
  1313.4 18.8 copy-start.31
  1313.4 18.8 copy-start.35
  1313.4 18.8 copy-start.38
  1324.4 7.9 all-to-all-start.7
  1327.8 538.5 %reduce-scatter.5.cloned.1.call-start = ((), (), s32[]{:S(2)}) async-start(), calls=%async_computation.26 | async-start | bytes 29020160
  1341.7 9.1 copy-start.6
  1341.7 9.1 copy-start.11
  1341.7 9.1 copy-start.45
  1341.7 11.2 copy-start.32
  1379.1 13.1 copy-start.29
  1379.1 14.7 copy-start.28
  1379.1 16.2 copy-start.27
  1396.9 28.7 %copy-start.26 = (f32[64,48]{1,0:T(8,128)S(1)}, f32[64,48]{1,0:T(8,128)}, u32[]{:S(2)}) copy-start(f32[64,48]{1,0:T(8,128)} %reshape.497) | copy-start | bytes 36868
  1873.7 5.7 all-to-all-start.15
  1880.0 5.7 all-to-all-start.14
  1886.2 5.7 all-to-all-start.13
  1892.5 5.7 all-to-all-start.9
  1898.8 5.7 all-to-all-start.8
  1905.1 5.7 all-to-all-start.11
  1911.3 5.7 all-to-all-start.17
  1917.7 6.2 all-to-all-start.12
  1924.5 6.8 all-to-all-start.10
  1932.0 7.1 all-to-all-start.16
  1939.8 6.8 all-to-all-start.18
  (150 other events, 344.2 us)
Sparse Core Ops, SparseCore 0:
  11.8 77.0 all-gather.13
  92.6 73.0 all-gather.9
  169.5 80.9 all-gather.15
  254.1 130.8 all-gather.7
  473.8 294.2 all-gather.11
  1498.8 367.3 reduce-scatter.4
where the time goes:
time: 1990 us; the launch traced here: 1950 us
  blocking collectives  631 us (32%)
  waiting for transfers between devices  543 us (27%)
  local copies, waits for them, and re-layouts  380 us (19%)
  matrix products  290 us (15%)
  starting transfers between devices  57.8 us (3%)
  other arithmetic  34.3 us (2%)
    all_gather x1, blocking collectives, in_one_piece(): filled = lax.all_gather(both, axis, axis=dim, tiled=True)  445 us
    unnamed x7, waiting for transfers between devices  360 us
    unnamed x1, blocking collectives  168 us
    unnamed x114, local copies, waits for them, and re-layouts  127 us
    all_gather x2, waiting for transfers between devices, in_one_piece(): filled = lax.all_gather(both, axis, axis=dim, tiled=True)  124 us
    dot_general x32, matrix products, key_step(): jnp.einsum('hqk,qhd->khd', grad_scores, query_blk, preferred_element_type...  115 us
    split x7, local copies, waits for them, and re-layouts, in_one_piece(): jnp.split(filled, [sum(widths[:k]) for k in range(1, len(widths))], axis=...  101 us
    dot_general x32, matrix products, key_step(): jnp.einsum('hqk,qhd->khd', weights, grad_blk, preferred_element_type=jnp....  63.6 us
  transfers between devices with their start and end apart: 23, of which 18 were waited for; matrix products, arithmetic and copies ran while one was open for 22% of the time, Pallas kernels for 0%

commit v1 on v0

v1 whole, which is shorter than its diff:
```python
import jax
import jax.numpy as jnp
from jax import lax
from jax.experimental import pallas as pl
from jax.experimental.pallas import tpu as pltpu
from jax.sharding import Mesh
from jax.sharding import PartitionSpec as P

D = 768
HEAD_DIM = 64
EPS = 1e-05
NEG = -1e30
LOG2E = 1.4426950408889634
F32 = jnp.float32
BF16 = jnp.bfloat16
HALF = 256
GROUPS = 32
BLOCKS = 2 * GROUPS
LOCAL = 192
VMEM_BYTES = 48 * 1024 * 1024
TEAM = ("c", "h")
SWAP = [(0, 1), (1, 0)]
MIRROR = [(i, GROUPS - 1 - i) for i in range(GROUPS)]
SMALL = (12, 12, 24, 12, 12, 12, 48, 12)


def matmul(left, right):
    return jnp.dot(left, right, preferred_element_type=F32)


def trans_left(left, right):
    return lax.dot_general(left, right, (((0,), (0,)), ((), ())), preferred_element_type=F32)


def trans_right(left, right):
    return lax.dot_general(left, right, (((1,), (1,)), ((), ())), preferred_element_type=F32)


def layer_norm(values, gain, shift):
    mean = jnp.mean(values, axis=-1, keepdims=True)
    centred = values - mean
    spread = jnp.mean(centred * centred, axis=-1, keepdims=True)
    return centred * lax.rsqrt(spread + EPS) * gain + shift


def gelu_tanh(values):
    return jax.nn.gelu(values, approximate=True)


def team_others(parts):
    return (
        lax.ppermute(parts[0], "h", SWAP),
        lax.ppermute(parts[1], "c", SWAP),
        lax.ppermute(parts[2], TEAM, [(i, 3 - i) for i in range(4)]),
    )


def team_gather(own):
    c, h = lax.axis_index("c"), lax.axis_index("h")
    by_h, by_c, by_both = team_others((own, own, own))
    near = (jnp.where(h == 0, own, by_h), jnp.where(h == 0, by_h, own))
    far = (jnp.where(h == 0, by_c, by_both), jnp.where(h == 0, by_both, by_c))
    low = [jnp.where(c == 0, a, b) for a, b in zip(near, far)]
    high = [jnp.where(c == 0, b, a) for a, b in zip(near, far)]
    return low + high


def team_scatter_sum(partial):
    rank = 2 * lax.axis_index("c") + lax.axis_index("h")
    rows = partial.shape[0] // 4

    def piece(k):
        return lax.dynamic_slice_in_dim(partial, (rank ^ k) * rows, rows, 0)

    others = team_others(tuple(piece(k).astype(BF16) for k in (1, 2, 3)))
    return piece(0) + sum(o.astype(F32) for o in others)


def block_row(b):
    return pl.multiple_of(512 * (b % GROUPS) + HALF * (b // GROUPS), HALF)


def nt(left, right):
    return lax.dot_general(left, right, (((1,), (1,)), ((), ())), preferred_element_type=F32)


def diagonal():
    key = lax.broadcasted_iota(jnp.int32, (HALF, HALF), 0)
    query = lax.broadcasted_iota(jnp.int32, (HALF, HALF), 1)
    return key <= query


def forward_kernel(g_ref, q_ref, kv_ref, att_ref, lse_ref, top, total, accum):
    g = g_ref[0]
    for slot, own in ((0, g), (1, BLOCKS - 1 - g)):
        top[...] = jnp.full_like(top, NEG)
        total[...] = jnp.zeros_like(total)
        accum[...] = jnp.zeros_like(accum)
        span = pl.ds(slot * HALF, HALF)

        def tile(b, masked):
            rows = pl.ds(block_row(b), HALF)
            first, second, third = (kv_ref[rows, pl.ds(128 * k, 128)] for k in range(3))
            second_t, third_t = second.T, third.T
            values = (second_t[64:], third_t[:64], third_t[64:])
            for h, keys in enumerate((first, first, second)):
                scores = nt(keys, q_ref[h, span, :])
                if masked:
                    scores = jnp.where(diagonal(), scores, NEG)
                line = pl.ds(h, 1)
                old = top[line, :]
                new = jnp.maximum(old, jnp.max(scores, axis=0, keepdims=True))
                weights = jnp.exp(scores - new)
                fade = jnp.exp(old - new)
                top[line, :] = new
                total[line, :] = total[line, :] * fade + jnp.sum(weights, axis=0, keepdims=True)
                accum[h] = accum[h] * fade + matmul(values[h], weights.astype(BF16))

        lax.fori_loop(0, own, lambda b, _: (tile(b, False), 0)[1], 0)
        tile(own, True)
        for h in range(3):
            line = pl.ds(h, 1)
            att_ref[slot, pl.ds(64 * h, 64), :] = accum[h] / total[line, :]
        lse_ref[:, span] = (top[...] + jnp.log(jnp.maximum(total[...], 1e-30))) * LOG2E


def query_kernel(g_ref, q_ref, do_ref, st_ref, kv_ref, dq_ref, accum):
    g = g_ref[0]
    for slot, own in ((0, g), (1, BLOCKS - 1 - g)):
        accum[...] = jnp.zeros_like(accum)
        span = pl.ds(slot * HALF, HALF)

        def tile(b, masked):
            rows = pl.ds(block_row(b), HALF)
            first, second, third = (kv_ref[rows, pl.ds(128 * k, 128)] for k in range(3))
            first_t, second_t = first.T, second.T
            keys_t = (first_t[:64], first_t[64:], second_t[:64])
            for h, (keys, values) in enumerate(
                ((first, second), (first, third), (second, third))
            ):
                scores = nt(keys, q_ref[h, span, :]) * LOG2E - st_ref[pl.ds(h, 1), span]
                if masked:
                    scores = jnp.where(diagonal(), scores, NEG)
                pull = nt(values, do_ref[h, span, :]) - st_ref[pl.ds(3 + h, 1), span]
                grad = (jnp.exp2(scores) * pull).astype(BF16)
                accum[h] += matmul(keys_t[h], grad)

        lax.fori_loop(0, own, lambda b, _: (tile(b, False), 0)[1], 0)
        tile(own, True)
        for h in range(3):
            dq_ref[slot, pl.ds(64 * h, 64), :] = accum[h] * 0.125


def key_kernel(g_ref, k_ref, v_ref, q_ref, do_ref, st_ref, dk_ref, dv_ref, acc_k, acc_v):
    g = g_ref[0]
    for slot, own in ((0, g), (1, BLOCKS - 1 - g)):
        acc_k[...] = jnp.zeros_like(acc_k)
        acc_v[...] = jnp.zeros_like(acc_v)
        span = pl.ds(slot * HALF, HALF)

        def tile(b, masked):
            rows = pl.ds(block_row(b), HALF)
            device = jnp.where(b < GROUPS, b, BLOCKS - 1 - b)
            lanes = pl.ds(pl.multiple_of((b // GROUPS) * HALF, HALF), HALF)
            stats = st_ref[device, :, lanes]
            for h in range(3):
                part, width = (pl.ds(0, 128), 128) if h < 2 else (pl.ds(128, 64), 64)
                queries, grads = q_ref[rows, part], do_ref[rows, part]
                keys, values = k_ref[h, span, :width], v_ref[h, span, :width]
                scores = nt(keys, queries) * LOG2E - stats[h : h + 1]
                if masked:
                    scores = jnp.where(diagonal(), scores, NEG)
                weights = jnp.exp2(scores)
                pull = nt(values, grads) - stats[3 + h : 4 + h]
                acc_v[h, :, :width] += matmul(weights.astype(BF16), grads)
                acc_k[h, :, :width] += matmul((weights * pull).astype(BF16), queries)

        tile(own, True)
        lax.fori_loop(own + 1, BLOCKS, lambda b, _: (tile(b, False), 0)[1], 0)
        left = lax.broadcasted_iota(jnp.int32, (HALF, 128), 1) < 64
        for out, acc in ((dk_ref, acc_k), (dv_ref, acc_v)):
            out[span, pl.ds(0, 128)] = jnp.where(left, acc[0], acc[1]).astype(BF16)
            out[span, pl.ds(128, 64)] = acc[2, :, :64].astype(BF16)


def attention_call(kernel, outs, scratch, matmuls, *args):
    tiles = 65 * 3 * HALF * HALF
    count = len(args)
    return pl.pallas_call(
        kernel,
        out_shape=outs,
        in_specs=[pl.BlockSpec(memory_space=pltpu.SMEM)]
        + [pl.BlockSpec(memory_space=pltpu.VMEM)] * (count - 1),
        out_specs=[pl.BlockSpec(memory_space=pltpu.VMEM)] * len(outs),
        scratch_shapes=scratch,
        compiler_params=pltpu.CompilerParams(vmem_limit_bytes=VMEM_BYTES),
        cost_estimate=pl.CostEstimate(
            flops=tiles * 512 * matmuls,
            bytes_accessed=sum(a.size * a.dtype.itemsize for a in args),
            transcendentals=tiles,
        ),
    )(*args)


def swap_upper(value):
    return jnp.concatenate(
        [value[:HALF], lax.ppermute(value[HALF:], "g", MIRROR)], axis=0
    )


def side(value, h, right):
    part = value[:, 64 * h : 64 * h + 64]
    blank = jnp.zeros_like(part)
    return jnp.concatenate([blank, part] if right else [part, blank], axis=1)


def sides(value, places):
    return jnp.stack([side(value, h, right) for h, right in enumerate(places)])


def one_hot(rows, columns, row_of_column):
    row = lax.broadcasted_iota(jnp.int32, (rows, columns), 0)
    column = lax.broadcasted_iota(jnp.int32, (rows, columns), 1)
    return (row == row_of_column(column)).astype(BF16)


def natural_of(column):
    g, rest = column // 24, column % 24
    return 12 * (GROUPS * (rest // 12) + g) + rest % 12


def on_device(
    hidden_in,
    ln1_gain,
    ln1_shift,
    w_qkv,
    qv_bias,
    w_out,
    out_bias,
    ln2_gain,
    ln2_shift,
    w_fc,
    fc_bias,
    w_proj,
    proj_bias,
    out_grad,
):
    c, g, h = lax.axis_index("c"), lax.axis_index("g"), lax.axis_index("h")
    rank = 2 * c + h
    where_am_i = g.astype(jnp.int32)[None]

    tokens = jnp.concatenate(team_gather(jnp.concatenate([hidden_in, out_grad], axis=1)), axis=0)
    resid, cotangent = tokens[:, :D].astype(F32), tokens[:, D:]

    reorder = one_hot(D, D, natural_of)
    pick_units = one_hot(1536, D, lambda k: 48 * (k // 24) + 24 * h + k % 24)
    small = jnp.concatenate(
        [ln1_gain, ln1_shift, qv_bias, out_bias, ln2_gain, ln2_shift, fc_bias, proj_bias]
    )
    small = jnp.pad(small.reshape(12, 12), ((0, 0), (0, 116)))
    units = matmul(jnp.concatenate([w_fc[:, :1536], w_fc[:, 1536:]], axis=0), pick_units)
    units = units.astype(BF16)

    def columns_for(of_c):
        r = 2 * of_c + h
        qkv = [lax.dynamic_slice_in_dim(w_qkv, D * k + LOCAL * r, LOCAL, 1) for k in range(3)]
        fc = lax.dynamic_slice_in_dim(units, 12 * of_c, 12, 0)
        return jnp.concatenate([*qkv, small], axis=1), jnp.concatenate([fc, w_out], axis=1)

    mine, theirs = columns_for(c), columns_for(1 - c)

    def both(own, sent):
        other = lax.ppermute(sent, "c", SWAP)
        return jnp.concatenate(
            [jnp.where(c == 0, own, other), jnp.where(c == 0, other, own)], axis=0
        )

    first = lax.all_gather(both(mine[0], theirs[0]), "g", axis=0, tiled=True)
    proj_rows = lax.dynamic_slice_in_dim(w_proj, 24 * h, 24, 0)
    second = lax.all_gather(
        jnp.concatenate([both(mine[1], theirs[1]), proj_rows], axis=1), "g", axis=0, tiled=True
    )
    w_qkv_t = matmul(reorder, first[:, : 3 * LOCAL]).astype(BF16)
    rest = matmul(reorder, second[:, : 2 * D]).astype(BF16)
    w_fc_t, w_out_all, w_proj_t = rest[:, :D], rest[:, D:], second[:, 2 * D :]

    vectors = first[:, 3 * LOCAL : 3 * LOCAL + 12].reshape(GROUPS, 2, 144).astype(F32)
    vectors = vectors.transpose(1, 0, 2)
    cut, at = [], 0
    for width in SMALL:
        cut.append(vectors[:, :, at : at + width])
        at += width
    gain_one, shift_one, bias_qv, bias_out, gain_two, shift_two = (
        v.reshape(-1) for v in cut[:6]
    )
    bias_proj = cut[7].reshape(-1)
    bias_fc = lax.dynamic_slice_in_dim(
        lax.dynamic_index_in_dim(cut[6], c, 0, False), 24 * h, 24, 1
    ).reshape(-1)
    bias_q = lax.dynamic_slice_in_dim(bias_qv, LOCAL * rank, LOCAL, 0)
    bias_v = lax.dynamic_slice_in_dim(bias_qv, D + LOCAL * rank, LOCAL, 0)
    bias_here = jnp.concatenate([bias_q, jnp.zeros_like(bias_q), bias_v])

    normed1 = layer_norm(resid, gain_one, shift_one).astype(BF16)
    qkv = (matmul(normed1, w_qkv_t) + bias_here).astype(BF16)
    queries = qkv[:, :LOCAL] * jnp.asarray(0.125, BF16)
    kv_all = lax.all_gather(qkv[:, LOCAL:], "g", axis=0, tiled=True)
    query_all = lax.all_gather(queries, "g", axis=0, tiled=True)
    query_zz = sides(swap_upper(queries), (False, True, False))
    att_t, lse = attention_call(
        forward_kernel,
        [
            jax.ShapeDtypeStruct((2, LOCAL, HALF), F32),
            jax.ShapeDtypeStruct((8, 512), F32),
        ],
        [
            pltpu.VMEM((8, HALF), F32),
            pltpu.VMEM((8, HALF), F32),
            pltpu.VMEM((3, 64, HALF), F32),
        ],
        2,
        where_am_i,
        query_zz,
        kv_all,
    )
    attended = att_t.transpose(0, 2, 1).reshape(512, LOCAL).astype(BF16)
    attended = jnp.concatenate(team_gather(swap_upper(attended)), axis=1)

    mid = resid + matmul(attended, w_out_all) + bias_out
    normed2 = layer_norm(mid, gain_two, shift_two).astype(BF16)
    pre_fc = matmul(normed2, w_fc_t) + bias_fc
    activ = gelu_tanh(pre_fc).astype(BF16)
    grad_activ = trans_right(cotangent, w_proj_t)
    grad_pre = jax.vjp(gelu_tanh, pre_fc)[1](grad_activ)[0].astype(BF16)
    grad_norm2 = team_scatter_sum(trans_right(grad_pre, w_fc_t))
    own_rows = lambda v: lax.dynamic_slice_in_dim(v, 128 * rank, 128, 0)
    mid_own = own_rows(mid)
    grad_mid_ln, grad_gain2, grad_shift2 = jax.vjp(layer_norm, mid_own, gain_two, shift_two)[1](
        grad_norm2
    )
    grad_output = out_grad.astype(F32)
    grad_mid = grad_output + grad_mid_ln
    grad_attn = grad_mid.astype(BF16)
    grad_attn_all = jnp.concatenate(team_gather(grad_attn), axis=0)
    w_out_rows = lax.dynamic_slice_in_dim(w_out_all, LOCAL * rank, LOCAL, 0)
    grad_heads = trans_right(grad_attn_all, w_out_rows).astype(BF16)
    grad_heads_all = lax.all_gather(grad_heads, "g", axis=0, tiled=True)
    grad_zz = swap_upper(grad_heads)
    grad_zz_t = grad_zz.reshape(2, HALF, LOCAL).transpose(0, 2, 1)
    delta = jnp.sum((grad_zz_t.astype(F32) * att_t).reshape(2, 3, 64, HALF), axis=2)
    delta = delta.transpose(1, 0, 2).reshape(3, 512)
    stats = jnp.concatenate([lse[:3], delta, jnp.zeros((2, 512), F32)], axis=0)
    stats_all = lax.all_gather(stats, "g", axis=0, tiled=False)

    output = mid_own + bias_proj + team_scatter_sum(matmul(activ, w_proj_t))
    hidden_out = output.astype(BF16)

    (dq_t,) = attention_call(
        query_kernel,
        [jax.ShapeDtypeStruct((2, LOCAL, HALF), F32)],
        [pltpu.VMEM((3, 64, HALF), F32)],
        3,
        where_am_i,
        query_zz,
        sides(grad_zz, (True, False, True)),
        stats,
        kv_all,
    )
    def kv_rows(b):
        return lax.dynamic_slice_in_dim(kv_all, 512 * (b % GROUPS) + HALF * (b // GROUPS), HALF, 0)

    kv_zz = jnp.concatenate([kv_rows(g), kv_rows(BLOCKS - 1 - g)], axis=0)
    dk, dv = attention_call(
        key_kernel,
        [jax.ShapeDtypeStruct((512, LOCAL), BF16)] * 2,
        [pltpu.VMEM((3, HALF, 128), F32)] * 2,
        4,
        where_am_i,
        sides(kv_zz[:, :LOCAL], (False, True, False)),
        sides(kv_zz[:, LOCAL:], (False, True, False)),
        query_all,
        grad_heads_all,
        stats_all,
    )
    grad_q = swap_upper(dq_t.transpose(0, 2, 1).reshape(512, LOCAL).astype(BF16))
    grad_kv = swap_upper(jnp.concatenate([dk, dv], axis=1))
    grad_qkv = jnp.concatenate([grad_q, grad_kv], axis=1)
    grad_norm1 = team_scatter_sum(trans_right(grad_qkv, w_qkv_t))
    resid_own = hidden_in.astype(F32)
    grad_in_ln, grad_gain1, grad_shift1 = jax.vjp(layer_norm, resid_own, gain_one, shift_one)[1](
        grad_norm1
    )
    input_grad = grad_mid + grad_in_ln

    def reordered(v):
        return matmul(v, reorder).astype(BF16)

    grad_wfc = trans_left(reordered(normed2), grad_pre)
    grad_attn_cols = lax.dynamic_slice_in_dim(grad_attn_all, LOCAL * rank, LOCAL, 1)
    grad_wout = trans_left(reordered(attended), grad_attn_cols)
    grad_wproj = trans_left(activ, cotangent)
    grad_wqkv = trans_left(reordered(normed1), grad_qkv)

    def sum_over_g(value):
        lines = value.astype(BF16).reshape(GROUPS, 24, value.shape[-1])
        lines = lax.all_to_all(lines, "g", 0, 0, tiled=True)
        return jnp.sum(lines.astype(F32), axis=0)

    late = jnp.concatenate([grad_wfc, grad_wout, grad_wproj], axis=1)
    late = sum_over_g(late)

    def spread(vector):
        return vector.reshape(2, GROUPS, -1)

    grad_qkv_sum = jnp.sum(grad_qkv.astype(F32), axis=0)
    qv_sums = jnp.zeros((2, 4, LOCAL), F32)
    qv_sums = lax.dynamic_update_slice(
        qv_sums,
        jnp.stack([grad_qkv_sum[:LOCAL], grad_qkv_sum[2 * LOCAL :]])[:, None],
        (0, rank, 0),
    ).reshape(-1)
    fc_sums = jnp.sum(grad_pre.astype(F32), axis=0).reshape(1, GROUPS, 24)
    fc_sums = lax.dynamic_update_slice(
        jnp.zeros((2, GROUPS, 48), F32), fc_sums, (c, jnp.int32(0), 24 * h)
    )
    small_sums = jnp.concatenate(
        [
            spread(grad_gain1),
            spread(grad_shift1),
            spread(qv_sums),
            spread(jnp.sum(grad_attn.astype(F32), axis=0)),
            spread(grad_gain2),
            spread(grad_shift2),
            fc_sums,
            spread(jnp.sum(grad_output, axis=0)),
        ],
        axis=2,
    )
    small_sums = small_sums.transpose(1, 0, 2).reshape(GROUPS * 24, 12)
    small_sums = jnp.pad(small_sums, ((0, 0), (0, 52)))
    early = sum_over_g(jnp.concatenate([grad_wqkv, small_sums], axis=1))

    final = jnp.concatenate([early, late], axis=1).astype(BF16)
    pieces = [p.astype(F32) for p in team_gather(final)]
    mine = [lax.dynamic_slice_in_dim(p, 12 * c, 12, 0) for p in pieces]
    total_wqkv = jnp.concatenate(
        [mine[t][:, LOCAL * k : LOCAL * (k + 1)] for k in range(3) for t in range(4)], axis=1
    )
    total_small = sum(mine)[:, 576:588].reshape(144)
    fc_pieces = jnp.stack([m[:, 640 : 640 + D] for m in mine])
    total_wfc = fc_pieces.reshape(2, 2, 12, GROUPS, 24).transpose(2, 0, 3, 1, 4).reshape(12, 3072)
    total_wout = jnp.concatenate([m[:, 640 + D : 640 + D + LOCAL] for m in mine], axis=1)
    proj_pieces = jnp.stack([p[:, 640 + D + LOCAL :] for p in pieces])
    total_wproj = lax.dynamic_slice_in_dim(proj_pieces, 2 * c, 2, 0).reshape(48, D)
    smalls, at = [], 0
    for width in SMALL:
        smalls.append(total_small[at : at + width])
        at += width
    return (
        hidden_out,
        input_grad,
        smalls[0],
        smalls[1],
        total_wqkv,
        smalls[2],
        total_wout,
        smalls[3],
        smalls[4],
        smalls[5],
        total_wfc,
        smalls[6],
        total_wproj,
        smalls[7],
    )


def solution(mesh):
    cut = Mesh(mesh.devices.reshape(2, GROUPS, 2), ("c", "g", "h"))
    tokens, rows, line = P(("c", "g", "h"), None), P(("c", "g"), None), P(("c", "g"))
    in_specs = (
        tokens, line, line, rows, line, rows, line, line, line, rows, line, rows, line, tokens,
    )
    out_specs = (
        tokens, tokens, line, line, rows, line, rows, line, line, line, rows, line, rows, line,
    )
    return jax.shard_map(
        on_device, mesh=cut, in_specs=in_specs, out_specs=out_specs, check_vma=False
    )
```

time: 1990 us -> 553 us (0.28); the launches traced: 1950 us -> 544 us
  blocking collectives: 631 us -> 23.1 us
  waiting for transfers between devices: 543 us -> 155 us
  local copies, waits for them, and re-layouts: 380 us -> 45.1 us
  matrix products: 290 us -> 30.2 us
  Pallas kernels: 0 us -> 183 us
    all_gather x1, blocking collectives: 445 us -> 23.1 us  [on_device(): stats_all = lax.all_gather(stats, 'g', axis=0, tiled=False)]
    unnamed x7 -> x5, waiting for transfers between devices: 360 us -> 0.08 us
    dot_general x104 -> x7, matrix products: 256 us -> 11 us  [matmul(): return jnp.dot(left, right, preferred_element_type=F32)]
    pallas_call x0 -> x3, Pallas kernels: none -> 183 us  [attention_call(): pl.pallas_call(kernel, out_shape=outs, in_specs=[pl.BlockSpec(memory_spac...]
    unnamed x1 -> x0, blocking collectives: 168 us -> none
    unnamed x114 -> x121, local copies, waits for them, and re-layouts: 127 us -> 8.21 us
    split x7 -> x0, local copies, waits for them, and re-layouts: 101 us -> none  [in_one_piece(): jnp.split(filled, [sum(widths[:k]) for k in range(1, len(widths))], axis=...]
    all_gather x5, waiting for transfers between devices: 142 us -> 71.9 us  [the longest x1 46 us: on_device(): kv_all = lax.all_gather(qkv[:, LOCAL:], 'g', axis=0, tiled=True)]
  transfers between devices with their start and end apart: 23 -> 35, of which waited for: 18 -> 22; matrix products, arithmetic and copies ran while one was open for 22% -> 14% of each run, Pallas kernels for 0% -> 34%
where the time goes in v1:
time: 553 us; the launch traced here: 544 us
  Pallas kernels  183 us (33%)
  waiting for transfers between devices  155 us (28%)
  starting transfers between devices  63.2 us (11%)
  local copies, waits for them, and re-layouts  45.1 us (8%)
  matrix products  30.2 us (5%)
  other arithmetic  28.2 us (5%)
  blocking collectives  23.1 us (4%)
  between operations  15.5 us (3%)
    pallas_call x3, Pallas kernels, attention_call(): pl.pallas_call(kernel, out_shape=outs, in_specs=[pl.BlockSpec(memory_spac...  183 us
    all_gather x1, waiting for transfers between devices, on_device(): kv_all = lax.all_gather(qkv[:, LOCAL:], 'g', axis=0, tiled=True)  46 us
    ppermute x7, waiting for transfers between devices, team_others(): lax.ppermute(parts[1], 'c', SWAP)  30.6 us
    all_gather x1, waiting for transfers between devices, on_device(): first = lax.all_gather(both(mine[0], theirs[0]), 'g', axis=0, tiled=True)  25.9 us
    all_gather x1, blocking collectives, on_device(): stats_all = lax.all_gather(stats, 'g', axis=0, tiled=False)  23.1 us
    ppermute x5, starting transfers between devices, swap_upper(): lax.ppermute(value[HALF:], 'g', MIRROR)  17.8 us
    ppermute x7, starting transfers between devices, team_others(): lax.ppermute(parts[1], 'c', SWAP)  16.4 us
    ppermute x5, waiting for transfers between devices, swap_upper(): lax.ppermute(value[HALF:], 'g', MIRROR)  16.1 us
  transfers between devices with their start and end apart: 35, of which 22 were waited for; matrix products, arithmetic and copies ran while one was open for 14% of the time, Pallas kernels for 34%

profile of v1, /device:TPU:1, one launch (start us, length us, event | category | flops | bytes accessed | tf_op | source)
XLA Modules:
  0.0 543.7 jit_solution(8274060431348439957)
XLA Ops:
  7.3 5.4 concatenate.141
  13.8 3.6 collective-permute-start.3
  21.8 2.4 collective-permute-start.1
  24.4 4.6 collective-permute-done
  29.0 11.0 %collective-permute-done.1 = bf16[128,1536]{1,0:T(8,128)(2,1)S(1)} collective-permute-done((bf16[128,1536]{1,0:T(8,128)(2,1)S(1)}, bf16[128,1536]{1,0:T(8,128)(2,1)S(1)}, u32[]{:S(2)}, u32[]{:S(2)}) %collective-permute-start.1) | collective-permute-done | bytes 393248 | tf_op jit(solution)/shard_map/ppermute | solution.py:53
  40.9 25.9 %all-gather.7.cloned.1.call-done = bf16[768,704]{1,0:T(8,128)(2,1)} async-done(((bf16[24,704]{1,0:T(8,128)(2,1)}), bf16[768,704]{1,0:T(8,128)(2,1)}) %all-gather.7.cloned.1.call-update) | async-done | bytes 1081360 | tf_op jit(solution)/shard_map/all_gather | solution.py:278
  68.8 2.2 convolution_convert_fusion.4
  74.1 2.8 collective-permute-start.9
  81.2 3.7 collective-permute-start.4
  85.0 6.9 %collective-permute-done.4 = bf16[256,192]{1,0:T(8,128)(2,1)S(1)} collective-permute-done((bf16[256,192]{1,0:T(8,128)(2,1)S(1)}, bf16[256,192]{1,0:T(8,128)(2,1)S(1)}, u32[]{:S(2)}, u32[]{:S(2)}) %collective-permute-start.4) | collective-permute-done | bytes 98336 | tf_op jit(solution)/shard_map/ppermute | solution.py:207
  92.1 46.0 %all-gather.9.cloned.1.call-done.kv_ref = bf16[16384,384]{1,0:T(8,128)(2,1)} async-done(((bf16[512,384]{1,0:T(8,128)(2,1)}), bf16[16384,384]{1,0:T(8,128)(2,1)}) %all-gather.9.cloned.1.call-update) | async-done | bytes 12582928 | tf_op jit(solution)/shard_map/all_gather | solution.py:307
  139.9 65.7 %shard_map.245 = (f32[2,192,256]{2,1,0:T(8,128)S(1)}, f32[8,512]{1,0:T(8,128)S(1)}) custom-call(s32[1]{0:T(128)} %bitcast.g_ref, bf16[3,512,128]{2,1,0:T(8,128)(2,1)S(1)} %pad_maximum_fusion.4.q_ref, bf16[16384,384]{1,0:T(8,128)(2,1)} %all-gather.9.cloned.1.call-done.kv_ref), custom_call_target="tpu_custom_call" | custom-call | flops 13086228480 | bytes 12976132 | tf_op jit(solution)/shard_map/pallas_call | solution.py:189
  205.7 2.9 collective-permute-start.5
  209.3 5.1 collective-permute-done.5
  215.7 2.4 collective-permute-start.7
  218.6 3.9 convolution_convert_fusion
  222.5 4.6 collective-permute-done.7
  227.1 2.6 collective-permute-done.8
  238.9 2.5 collective-permute-start.15
  244.3 2.6 collective-permute-start.12
  251.0 4.0 collective-permute-done.11
  255.0 3.1 collective-permute-done.12
  260.0 3.8 collective-permute-start.17
  264.5 6.5 %collective-permute-done.17 = bf16[128,768]{1,0:T(8,128)(2,1)S(1)} collective-permute-done((bf16[128,768]{1,0:T(8,128)(2,1)S(1)}, bf16[128,768]{1,0:T(8,128)(2,1)S(1)}, u32[]{:S(2)}, u32[]{:S(2)}) %collective-permute-start.17) | collective-permute-done | bytes 196640 | tf_op jit(solution)/shard_map/ppermute | solution.py:53
  271.7 3.0 collective-permute-done.18
  279.5 2.0 convolution_convert_fusion.1
  281.6 4.6 convolution_convert_fusion.2
  287.8 4.3 collective-permute-start.19
  292.1 2.2 pad_maximum_fusion.3
  294.3 3.3 fusion.38
  297.6 1.9 copy.100
  299.5 5.7 %concatenate.181 = bf16[32,24,1728]{2,1,0:T(8,128)(2,1)} concatenate(bf16[32,24,768]{2,1,0:T(8,128)(2,1)} %bitcast.100, bf16[32,24,192]{2,1,0:T(8,128)(2,1)} %bitcast.98, bf16[32,24,768]{2,1,0:T(8,128)(2,1)} %bitcast.99), dimensions={2} | concatenate | bytes 5308416 | tf_op jit(solution)/shard_map/concatenate | solution.py:409
  305.2 4.6 all-to-all-start.1
  317.7 57.6 %shard_map.246 = f32[2,192,256]{2,1,0:T(8,128)S(1)} custom-call(s32[1]{0:T(128)} %bitcast.g_ref, bf16[3,512,128]{2,1,0:T(8,128)(2,1)S(1)} %pad_maximum_fusion.4.q_ref, bf16[3,512,128]{2,1,0:T(8,128)(2,1)S(1)} %pad_maximum_fusion.5.do_ref, f32[8,512]{1,0:T(8,128)S(1)} %maximum_maximum_fusion.1.st_ref, bf16[16384,384]{1,0:T(8,128)(2,1)} %all-gather.9.cloned.1.call-done.kv_ref), custom_call_target="tpu_custom_call" | custom-call | flops 19629342720 | bytes 13385732 | tf_op jit(solution)/shard_map/pallas_call | solution.py:189
  376.2 4.4 collective-permute-start.20
  380.6 23.1 %all-gather = f32[256,512]{1,0:T(8,128)S(1)} all-gather(f32[8,512]{1,0:T(8,128)S(1)} %maximum_maximum_fusion.1.st_ref), channel_id=2, replica_groups=mesh['c'=2,'g'=32,'h'=2] {'g'}, dimensions={0}, use_global_device_ids=true | all-gather | bytes 540672 | tf_op jit(solution)/shard_map/all_gather | solution.py:353
  403.8 59.6 %shard_map.247 = (bf16[512,192]{1,0:T(8,128)(2,1)S(1)}, bf16[512,192]{1,0:T(8,128)(2,1)S(1)}) custom-call(s32[1]{0:T(128)} %bitcast.g_ref, bf16[3,512,128]{2,1,0:T(8,128)(2,1)S(1)} %pad_maximum_fusion.6.k_ref, bf16[3,512,128]{2,1,0:T(8,128)(2,1)S(1)} %pad_maximum_fusion.7.v_ref, bf16[16384,192]{1,0:T(8,128)(2,1)} %all-gather.13.cloned.1.call-done.q_ref, ...), custom_call_target="tpu_custom_call" | custom-call | flops 26172456960 | bytes 13893636 | tf_op jit(solution)/shard_map/pallas_call | solution.py:189
  463.6 2.5 collective-permute-start.21
  469.2 4.2 collective-permute-done.21
  473.4 2.1 fusion.115
  478.7 2.6 collective-permute-start.24
  482.6 3.8 convolution_convert_fusion.3
  493.8 5.9 %all-to-all-start = ((bf16[32,24,640]{2,1,0:T(8,128)(2,1)}), bf16[32,24,640]{2,1,0:T(8,128)(2,1)S(1)}, u32[]{:S(2)}, u32[]{:S(2)}) async-start(bf16[32,24,640]{2,1,0:T(8,128)(2,1)} %pad_maximum_fusion.1), calls=%async_computation | async-start | bytes 1966080 | tf_op jit(solution)/shard_map/all_to_all | solution.py:406
  499.7 2.2 reduce.3
  502.0 13.9 %all-to-all-done = bf16[32,24,640]{2,1,0:T(8,128)(2,1)S(1)} async-done(((bf16[32,24,640]{2,1,0:T(8,128)(2,1)}), bf16[32,24,640]{2,1,0:T(8,128)(2,1)S(1)}, u32[]{:S(2)}, u32[]{:S(2)}) %all-to-all-start) | async-done | bytes 983072 | tf_op jit(solution)/shard_map/all_to_all | solution.py:406
  516.1 3.8 collective-permute-start.26
  521.2 4.5 collective-permute-done.26
  525.7 2.7 collective-permute-done.27
  (336 shorter events, 79.3 us)
Async XLA Ops:
  7.2 69.7 %copy-start = (bf16[48,768]{1,0:T(8,128)(2,1)S(1)}, bf16[48,768]{1,0:T(8,128)(2,1)}, u32[]{:S(2)}) copy-start(bf16[48,768]{1,0:T(8,128)(2,1)} %param.25) | copy-start | bytes 221188
  7.2 59.6 %all-gather.7.cloned.1.call-start = ((), (), s32[]{:S(2)}) async-start(), calls=%async_computation.2 | async-start | bytes 1216512 | tf_op jit(solution)/shard_map/all_gather | solution.py:278
  13.8 4.8 collective-permute-start.3
  19.3 118.7 %all-gather.9.cloned.1.call-start = ((), (), s32[]{:S(2)}) async-start(), calls=%async_computation.3 | async-start | bytes 12976128 | tf_op jit(solution)/shard_map/all_gather | solution.py:307
  20.3 8.7 %collective-permute-start = (bf16[128,1536]{1,0:T(8,128)(2,1)S(1)}, bf16[128,1536]{1,0:T(8,128)(2,1)S(1)}, u32[]{:S(2)}, u32[]{:S(2)}) collective-permute-start(bf16[128,1536]{1,0:T(8,128)(2,1)S(1)} %constant_dynamic-update-slice_fusion), channel_id=1, source_target_pairs={{0,1},{1,0},{2,3},{3,2},{4,5},{5,4},{6,7},{7,6},{8,9},{9,8},{10,11... | collective-permute-start | bytes 1179656 | tf_op jit(solution)/shard_map/ppermute | solution.py:52
  21.8 18.2 %collective-permute-start.1 = (bf16[128,1536]{1,0:T(8,128)(2,1)S(1)}, bf16[128,1536]{1,0:T(8,128)(2,1)S(1)}, u32[]{:S(2)}, u32[]{:S(2)}) collective-permute-start(bf16[128,1536]{1,0:T(8,128)(2,1)S(1)} %constant_dynamic-update-slice_fusion), channel_id=1, source_target_pairs={{0,64},{64,0},{1,65},{65,1},{2,66},{66,2},{3,67},{67,3},{4,68},{68... | collective-permute-start | bytes 1179656 | tf_op jit(solution)/shard_map/ppermute | solution.py:53
  24.3 15.8 %collective-permute-start.2 = (bf16[128,1536]{1,0:T(8,128)(2,1)S(1)}, bf16[128,1536]{1,0:T(8,128)(2,1)S(1)}, u32[]{:S(2)}, u32[]{:S(2)}) collective-permute-start(bf16[128,1536]{1,0:T(8,128)(2,1)S(1)} %constant_dynamic-update-slice_fusion), channel_id=1, source_target_pairs={{0,65},{1,64},{64,1},{65,0},{2,67},{3,66},{66,3},{67,2},{4,69},{5,... | collective-permute-start | bytes 1179656 | tf_op jit(solution)/shard_map/ppermute | solution.py:54
  24.3 194.2 %copy-start.48 = (pred[768]{0:T(1024)(128)(4,1)}, pred[768]{0:T(1024)(128)(4,1)S(1)}, u32[]{:S(2)}) copy-start(pred[768]{0:T(1024)(128)(4,1)S(1)} %get-tuple-element.140) | copy-start | bytes 2308
  24.3 194.2 %copy-start.51 = (pred[768]{0:T(1024)(128)(4,1)}, pred[768]{0:T(1024)(128)(4,1)S(1)}, u32[]{:S(2)}) copy-start(pred[768]{0:T(1024)(128)(4,1)S(1)} %get-tuple-element.141) | copy-start | bytes 2308
  24.3 194.2 %copy-start.32 = (s32[768]{0:T(1024)}, s32[768]{0:T(1024)S(1)}, u32[]{:S(2)}) copy-start(s32[768]{0:T(1024)S(1)} %get-tuple-element.142) | copy-start | bytes 9220
  24.4 194.2 %copy-start.35 = (s32[768]{0:T(1024)}, s32[768]{0:T(1024)S(1)}, u32[]{:S(2)}) copy-start(s32[768]{0:T(1024)S(1)} %get-tuple-element.143) | copy-start | bytes 9220
  24.4 194.2 %copy-start.38 = (s32[768]{0:T(1024)}, s32[768]{0:T(1024)S(1)}, u32[]{:S(2)}) copy-start(s32[768]{0:T(1024)S(1)} %get-tuple-element.144) | copy-start | bytes 9220
  24.4 194.2 %copy-start.41 = (s32[768]{0:T(1024)}, s32[768]{0:T(1024)S(1)}, u32[]{:S(2)}) copy-start(s32[768]{0:T(1024)S(1)} %get-tuple-element.145) | copy-start | bytes 9220
  40.9 30.2 %copy-start.44 = (f32[512]{0:T(512)}, f32[512]{0:T(512)S(1)}, u32[]{:S(2)}) copy-start(f32[512]{0:T(512)S(1)} %add_rsqrt_fusion.1) | copy-start | bytes 6148
  73.0 145.5 %all-gather.11.cloned.1.call-start = ((), (), s32[]{:S(2)}) async-start(), calls=%async_computation.4 | async-start | bytes 3649536 | tf_op jit(solution)/shard_map/all_gather | solution.py:280
  74.1 4.5 collective-permute-start.9
  78.7 60.4 %copy-start.54 = (pred[128]{0:T(512)(128)(4,1)S(1)}, pred[128]{0:T(512)(128)(4,1)}, u32[]{:S(2)}) copy-start(pred[128]{0:T(512)(128)(4,1)} %constant.160.clone.1) | copy-start | bytes 388
  79.4 324.3 %all-gather.13.cloned.1.call-start = ((), (), s32[]{:S(2)}) async-start(), calls=%async_computation.5 | async-start | bytes 8650752 | tf_op jit(solution)/shard_map/all_gather | solution.py:308
  80.2 323.6 %all-gather.15.cloned.1.call-start = ((), (), s32[]{:S(2)}) async-start(), calls=%async_computation.6 | async-start | bytes 8650752 | tf_op jit(solution)/shard_map/all_gather | solution.py:347
  81.2 10.6 %collective-permute-start.4 = (bf16[256,192]{1,0:T(8,128)(2,1)S(1)}, bf16[256,192]{1,0:T(8,128)(2,1)S(1)}, u32[]{:S(2)}, u32[]{:S(2)}) collective-permute-start(bf16[256,192]{1,0:T(8,128)(2,1)S(1)} %get-tuple-element.82), channel_id=1, source_target_pairs={{0,62},{2,60},{4,58},{6,56},{8,54},{10,52},{12,50},{14,48},{16,46}... | collective-permute-start | bytes 294920 | tf_op jit(solution)/shard_map/ppermute | solution.py:207
  205.7 8.7 %collective-permute-start.5 = (bf16[256,192]{0,1:T(8,128)(2,1)S(1)}, bf16[256,192]{0,1:T(8,128)(2,1)S(1)}, u32[]{:S(2)}, u32[]{:S(2)}) collective-permute-start(bf16[256,192]{0,1:T(8,128)(2,1)S(1)} %get-tuple-element.101), channel_id=1, source_target_pairs={{0,62},{2,60},{4,58},{6,56},{8,54},{10,52},{12,50},{14,48},{16,46}... | collective-permute-start | bytes 294920 | tf_op jit(solution)/shard_map/ppermute | solution.py:207
  208.9 23.6 %copy-start.30 = (f32[768]{0:T(1024)}, f32[768]{0:T(1024)S(1)}, u32[]{:S(2)}) copy-start(f32[768]{0:T(1024)S(1)} %add.408) | copy-start | bytes 9220
  214.4 8.1 %collective-permute-start.6 = (bf16[512,192]{0,1:T(8,128)(2,1)S(1)}, bf16[512,192]{0,1:T(8,128)(2,1)}, u32[]{:S(2)}, u32[]{:S(2)}) collective-permute-start(bf16[512,192]{0,1:T(8,128)(2,1)S(1)} %pad_maximum_fusion.10), channel_id=1, source_target_pairs={{0,1},{1,0},{2,3},{3,2},{4,5},{5,4},{6,7},{7,6},{8,9},{9,8},{10,11... | collective-permute-start | bytes 589832 | tf_op jit(solution)/shard_map/ppermute | solution.py:52
  215.7 11.4 %collective-permute-start.7 = (bf16[512,192]{0,1:T(8,128)(2,1)S(1)}, bf16[512,192]{0,1:T(8,128)(2,1)}, u32[]{:S(2)}, u32[]{:S(2)}) collective-permute-start(bf16[512,192]{0,1:T(8,128)(2,1)S(1)} %pad_maximum_fusion.10), channel_id=1, source_target_pairs={{0,64},{64,0},{1,65},{65,1},{2,66},{66,2},{3,67},{67,3},{4,68},{68... | collective-permute-start | bytes 589832 | tf_op jit(solution)/shard_map/ppermute | solution.py:53
  218.1 11.6 %collective-permute-start.8 = (bf16[512,192]{0,1:T(8,128)(2,1)S(1)}, bf16[512,192]{0,1:T(8,128)(2,1)}, u32[]{:S(2)}, u32[]{:S(2)}) collective-permute-start(bf16[512,192]{0,1:T(8,128)(2,1)S(1)} %pad_maximum_fusion.10), channel_id=1, source_target_pairs={{0,65},{1,64},{64,1},{65,0},{2,67},{3,66},{66,3},{67,2},{4,69},{5,... | collective-permute-start | bytes 589832 | tf_op jit(solution)/shard_map/ppermute | solution.py:54
  232.1 26.0 %copy-start.2 = (f32[512,768]{1,0:T(8,128)}, f32[512,768]{1,0:T(8,128)S(1)}, u32[]{:S(2)}) copy-start(f32[512,768]{1,0:T(8,128)S(1)} %get-tuple-element.137) | copy-start | bytes 4718596
  237.5 6.9 %collective-permute-start.13 = (bf16[128,768]{1,0:T(8,128)(2,1)S(1)}, bf16[128,768]{1,0:T(8,128)(2,1)S(1)}, u32[]{:S(2)}, u32[]{:S(2)}) collective-permute-start(bf16[128,768]{1,0:T(8,128)(2,1)S(1)} %get-tuple-element.42), channel_id=1, source_target_pairs={{0,1},{1,0},{2,3},{3,2},{4,5},{5,4},{6,7},{7,6},{8,9},{9,8},{10,11... | collective-permute-start | bytes 589832 | tf_op jit(solution)/shard_map/ppermute | solution.py:52
  237.6 9.4 %collective-permute-start.14 = (bf16[128,768]{1,0:T(8,128)(2,1)S(1)}, bf16[128,768]{1,0:T(8,128)(2,1)S(1)}, u32[]{:S(2)}, u32[]{:S(2)}) collective-permute-start(bf16[128,768]{1,0:T(8,128)(2,1)S(1)} %get-tuple-element.44), channel_id=1, source_target_pairs={{0,64},{64,0},{1,65},{65,1},{2,66},{66,2},{3,67},{67,3},{4,68},{68... | collective-permute-start | bytes 589832 | tf_op jit(solution)/shard_map/ppermute | solution.py:53
  238.9 9.9 %collective-permute-start.15 = (bf16[128,768]{1,0:T(8,128)(2,1)S(1)}, bf16[128,768]{1,0:T(8,128)(2,1)S(1)}, u32[]{:S(2)}, u32[]{:S(2)}) collective-permute-start(bf16[128,768]{1,0:T(8,128)(2,1)S(1)} %get-tuple-element.43), channel_id=1, source_target_pairs={{0,65},{1,64},{64,1},{65,0},{2,67},{3,66},{66,3},{67,2},{4,69},{5,... | collective-permute-start | bytes 589832 | tf_op jit(solution)/shard_map/ppermute | solution.py:54
  242.6 8.5 %collective-permute-start.10 = (bf16[128,768]{1,0:T(8,128)(2,1)S(1)}, bf16[128,768]{1,0:T(8,128)(2,1)S(1)}, u32[]{:S(2)}, u32[]{:S(2)}) collective-permute-start(bf16[128,768]{1,0:T(8,128)(2,1)S(1)} %get-tuple-element.45), channel_id=1, source_target_pairs={{0,1},{1,0},{2,3},{3,2},{4,5},{5,4},{6,7},{7,6},{8,9},{9,8},{10,11... | collective-permute-start | bytes 589832 | tf_op jit(solution)/shard_map/ppermute | solution.py:52
  242.7 12.3 %collective-permute-start.11 = (bf16[128,768]{1,0:T(8,128)(2,1)S(1)}, bf16[128,768]{1,0:T(8,128)(2,1)S(1)}, u32[]{:S(2)}, u32[]{:S(2)}) collective-permute-start(bf16[128,768]{1,0:T(8,128)(2,1)S(1)} %get-tuple-element.47), channel_id=1, source_target_pairs={{0,64},{64,0},{1,65},{65,1},{2,66},{66,2},{3,67},{67,3},{4,68},{68... | collective-permute-start | bytes 589832 | tf_op jit(solution)/shard_map/ppermute | solution.py:53
  244.3 13.8 %collective-permute-start.12 = (bf16[128,768]{1,0:T(8,128)(2,1)S(1)}, bf16[128,768]{1,0:T(8,128)(2,1)S(1)}, u32[]{:S(2)}, u32[]{:S(2)}) collective-permute-start(bf16[128,768]{1,0:T(8,128)(2,1)S(1)} %get-tuple-element.46), channel_id=1, source_target_pairs={{0,65},{1,64},{64,1},{65,0},{2,67},{3,66},{66,3},{67,2},{4,69},{5,... | collective-permute-start | bytes 589832 | tf_op jit(solution)/shard_map/ppermute | solution.py:54
  259.9 4.6 collective-permute-start.16
  260.0 11.0 %collective-permute-start.17 = (bf16[128,768]{1,0:T(8,128)(2,1)S(1)}, bf16[128,768]{1,0:T(8,128)(2,1)S(1)}, u32[]{:S(2)}, u32[]{:S(2)}) collective-permute-start(bf16[128,768]{1,0:T(8,128)(2,1)S(1)} %get-tuple-element.31), channel_id=1, source_target_pairs={{0,64},{64,0},{1,65},{65,1},{2,66},{66,2},{3,67},{67,3},{4,68},{68... | collective-permute-start | bytes 589832 | tf_op jit(solution)/shard_map/ppermute | solution.py:53
  263.8 10.9 %collective-permute-start.18 = (bf16[128,768]{1,0:T(8,128)(2,1)S(1)}, bf16[128,768]{1,0:T(8,128)(2,1)}, u32[]{:S(2)}, u32[]{:S(2)}) collective-permute-start(bf16[128,768]{1,0:T(8,128)(2,1)S(1)} %get-tuple-element.31), channel_id=1, source_target_pairs={{0,65},{1,64},{64,1},{65,0},{2,67},{3,66},{66,3},{67,2},{4,69},{5,... | collective-permute-start | bytes 589832 | tf_op jit(solution)/shard_map/ppermute | solution.py:54
  287.8 22.0 %collective-permute-start.19 = (bf16[256,192]{1,0:T(8,128)(2,1)}, bf16[256,192]{1,0:T(8,128)(2,1)}, u32[]{:S(2)}, u32[]{:S(2)}) collective-permute-start(bf16[256,192]{1,0:T(8,128)(2,1)} %get-tuple-element.78), channel_id=1, source_target_pairs={{0,62},{2,60},{4,58},{6,56},{8,54},{10,52},{12,50},{14,48},{16,46}... | collective-permute-start | bytes 294920 | tf_op jit(solution)/shard_map/ppermute | solution.py:207
  305.2 188.6 %all-to-all-start.1 = ((bf16[32,24,1728]{2,1,0:T(8,128)(2,1)}), bf16[32,24,1728]{2,1,0:T(8,128)(2,1)}, u32[]{:S(2)}, u32[]{:S(2)}) async-start(bf16[32,24,1728]{2,1,0:T(8,128)(2,1)} %concatenate.181), calls=%async_computation.1 | async-start | bytes 5505024 | tf_op jit(solution)/shard_map/all_to_all | solution.py:406
  376.2 93.0 %collective-permute-start.20 = (bf16[256,192]{1,0:T(8,128)(2,1)}, bf16[256,192]{1,0:T(8,128)(2,1)}, u32[]{:S(2)}, u32[]{:S(2)}) collective-permute-start(bf16[256,192]{1,0:T(8,128)(2,1)} %get-tuple-element.73), channel_id=1, source_target_pairs={{0,62},{2,60},{4,58},{6,56},{8,54},{10,52},{12,50},{14,48},{16,46}... | collective-permute-start | bytes 294920 | tf_op jit(solution)/shard_map/ppermute | solution.py:207
  403.8 65.3 %copy-start.26 = (bf16[768]{0:T(1024)(128)(2,1)S(1)}, bf16[768]{0:T(1024)(128)(2,1)}, u32[]{:S(2)}) copy-start(bf16[768]{0:T(1024)(128)(2,1)} %get-tuple-element.26) | copy-start | bytes 4612
  463.6 9.8 %collective-permute-start.21 = (bf16[256,384]{1,0:T(8,128)(2,1)S(1)}, bf16[256,384]{1,0:T(8,128)(2,1)S(1)}, u32[]{:S(2)}, u32[]{:S(2)}) collective-permute-start(bf16[256,384]{1,0:T(8,128)(2,1)S(1)} %get-tuple-element.61), channel_id=1, source_target_pairs={{0,62},{2,60},{4,58},{6,56},{8,54},{10,52},{12,50},{14,48},{16,46}... | collective-permute-start | bytes 589832 | tf_op jit(solution)/shard_map/ppermute | solution.py:207
  477.5 10.7 %collective-permute-start.22 = (bf16[128,768]{1,0:T(8,128)(2,1)}, bf16[128,768]{1,0:T(8,128)(2,1)S(1)}, u32[]{:S(2)}, u32[]{:S(2)}) collective-permute-start(bf16[128,768]{1,0:T(8,128)(2,1)} %get-tuple-element.38), channel_id=1, source_target_pairs={{0,1},{1,0},{2,3},{3,2},{4,5},{5,4},{6,7},{7,6},{8,9},{9,8},{10,11... | collective-permute-start | bytes 589832 | tf_op jit(solution)/shard_map/ppermute | solution.py:52
  477.5 10.7 %collective-permute-start.23 = (bf16[128,768]{1,0:T(8,128)(2,1)}, bf16[128,768]{1,0:T(8,128)(2,1)S(1)}, u32[]{:S(2)}, u32[]{:S(2)}) collective-permute-start(bf16[128,768]{1,0:T(8,128)(2,1)} %get-tuple-element.40), channel_id=1, source_target_pairs={{0,64},{64,0},{1,65},{65,1},{2,66},{66,2},{3,67},{67,3},{4,68},{68... | collective-permute-start | bytes 589832 | tf_op jit(solution)/shard_map/ppermute | solution.py:53
  478.7 11.2 %collective-permute-start.24 = (bf16[128,768]{1,0:T(8,128)(2,1)S(1)}, bf16[128,768]{1,0:T(8,128)(2,1)}, u32[]{:S(2)}, u32[]{:S(2)}) collective-permute-start(bf16[128,768]{1,0:T(8,128)(2,1)S(1)} %get-tuple-element.39), channel_id=1, source_target_pairs={{0,65},{1,64},{64,1},{65,0},{2,67},{3,66},{66,3},{67,2},{4,69},{5,... | collective-permute-start | bytes 589832 | tf_op jit(solution)/shard_map/ppermute | solution.py:54
  493.8 22.1 %all-to-all-start = ((bf16[32,24,640]{2,1,0:T(8,128)(2,1)}), bf16[32,24,640]{2,1,0:T(8,128)(2,1)S(1)}, u32[]{:S(2)}, u32[]{:S(2)}) async-start(bf16[32,24,640]{2,1,0:T(8,128)(2,1)} %pad_maximum_fusion.1), calls=%async_computation | async-start | bytes 1966080 | tf_op jit(solution)/shard_map/all_to_all | solution.py:406
  499.7 20.5 %copy-start.5 = (f32[128,768]{1,0:T(8,128)S(1)}, f32[128,768]{1,0:T(8,128)}, u32[]{:S(2)}) copy-start(f32[128,768]{1,0:T(8,128)} %copy-done.4) | copy-start | bytes 1179652
  516.0 5.1 collective-permute-start.25
  516.1 9.6 %collective-permute-start.26 = (bf16[24,2368]{1,0:T(8,128)(2,1)S(1)}, bf16[24,2368]{1,0:T(8,128)(2,1)S(1)}, u32[]{:S(2)}, u32[]{:S(2)}) collective-permute-start(bf16[24,2368]{1,0:T(8,128)(2,1)S(1)} %pad_maximum_fusion.15), channel_id=1, source_target_pairs={{0,64},{64,0},{1,65},{65,1},{2,66},{66,2},{3,67},{67,3},{4,68},{68... | collective-permute-start | bytes 341000 | tf_op jit(solution)/shard_map/ppermute | solution.py:53
  520.0 8.5 %collective-permute-start.27 = (bf16[24,2368]{1,0:T(8,128)(2,1)S(1)}, bf16[24,2368]{1,0:T(8,128)(2,1)S(1)}, u32[]{:S(2)}, u32[]{:S(2)}) collective-permute-start(bf16[24,2368]{1,0:T(8,128)(2,1)S(1)} %pad_maximum_fusion.15), channel_id=1, source_target_pairs={{0,65},{1,64},{64,1},{65,0},{2,67},{3,66},{66,3},{67,2},{4,69},{5,... | collective-permute-start | bytes 341000 | tf_op jit(solution)/shard_map/ppermute | solution.py:54
  (48 other events, 197.6 us)
Sparse Core Ops, SparseCore 0:
  19.4 47.2 all-gather.6
  73.1 64.8 all-gather.8
  140.9 45.5 all-gather.10
  188.7 53.6 all-gather.12
  277.9 82.9 all-gather.14

commit v2 on v1

--- a/solution.py
+++ b/solution.py
@@ -15,12 +15,16 @@
 BF16 = jnp.bfloat16
 HALF = 256
 GROUPS = 32
+TOKENS = 16384
 BLOCKS = 2 * GROUPS
 LOCAL = 192
 VMEM_BYTES = 48 * 1024 * 1024
 TEAM = ("c", "h")
 SWAP = [(0, 1), (1, 0)]
 MIRROR = [(i, GROUPS - 1 - i) for i in range(GROUPS)]
+MESH = pl.DeviceIdType.MESH
+GELU_ROOT = 0.7978845608028654
+GELU_CUBE = 0.044715
 SMALL = (12, 12, 24, 12, 12, 12, 48, 12)
 
 
@@ -90,93 +94,96 @@
     return key <= query
 
 
-def forward_kernel(g_ref, q_ref, kv_ref, att_ref, lse_ref, top, total, accum):
-    g = g_ref[0]
-    for slot, own in ((0, g), (1, BLOCKS - 1 - g)):
-        top[...] = jnp.full_like(top, NEG)
-        total[...] = jnp.zeros_like(total)
-        accum[...] = jnp.zeros_like(accum)
-        span = pl.ds(slot * HALF, HALF)
-
-        def tile(b, masked):
-            rows = pl.ds(block_row(b), HALF)
-            first, second, third = (kv_ref[rows, pl.ds(128 * k, 128)] for k in range(3))
-            second_t, third_t = second.T, third.T
-            values = (second_t[64:], third_t[:64], third_t[64:])
-            for h, keys in enumerate((first, first, second)):
-                scores = nt(keys, q_ref[h, span, :])
-                if masked:
-                    scores = jnp.where(diagonal(), scores, NEG)
-                line = pl.ds(h, 1)
-                old = top[line, :]
-                new = jnp.maximum(old, jnp.max(scores, axis=0, keepdims=True))
-                weights = jnp.exp(scores - new)
-                fade = jnp.exp(old - new)
-                top[line, :] = new
-                total[line, :] = total[line, :] * fade + jnp.sum(weights, axis=0, keepdims=True)
-                accum[h] = accum[h] * fade + matmul(values[h], weights.astype(BF16))
-
-        lax.fori_loop(0, own, lambda b, _: (tile(b, False), 0)[1], 0)
-        tile(own, True)
-        for h in range(3):
-            line = pl.ds(h, 1)
-            att_ref[slot, pl.ds(64 * h, 64), :] = accum[h] / total[line, :]
-        lse_ref[:, span] = (top[...] + jnp.log(jnp.maximum(total[...], 1e-30))) * LOG2E
-
-
-def query_kernel(g_ref, q_ref, do_ref, st_ref, kv_ref, dq_ref, accum):
+def span_loop(start, stop, width, tile):
+    count = stop - start
+    full = count // width
+    lax.fori_loop(0, full, lambda i, _: (tile([start + width * i + k for k in range(width)], False), 0)[1], 0)
+    if width > 1:
+        lax.fori_loop(start + full * width, stop, lambda b, _: (tile([b], False), 0)[1], 0)
+
+def cat(parts, axis=0):
+    return parts[0] if len(parts) == 1 else jnp.concatenate(parts, axis=axis)
+
+def query_kernel(g_ref, q_ref, do_ref, st_ref, kv_ref, dq_ref, accum, whole):
     g = g_ref[0]
     for slot, own in ((0, g), (1, BLOCKS - 1 - g)):
         accum[...] = jnp.zeros_like(accum)
         span = pl.ds(slot * HALF, HALF)
 
-        def tile(b, masked):
-            rows = pl.ds(block_row(b), HALF)
-            first, second, third = (kv_ref[rows, pl.ds(128 * k, 128)] for k in range(3))
+        def tile(blocks, masked):
+            rows = [pl.ds(block_row(b), HALF) for b in blocks]
+            first, second, third = (
+                cat([kv_ref[r, pl.ds(128 * k, 128)] for r in rows]) for k in range(3)
+            )
             first_t, second_t = first.T, second.T
             keys_t = (first_t[:64], first_t[64:], second_t[:64])
-            for h, (keys, values) in enumerate(
-                ((first, second), (first, third), (second, third))
-            ):
-                scores = nt(keys, q_ref[h, span, :]) * LOG2E - st_ref[pl.ds(h, 1), span]
+            raw = [
+                (nt(keys, q_ref[h, span, :]), nt(values, do_ref[h, span, :]))
+                for h, (keys, values) in enumerate(
+                    ((first, second), (first, third), (second, third))
+                )
+            ]
+            grads = []
+            for h, (scores, pull) in enumerate(raw):
+                scores = scores * LOG2E - st_ref[pl.ds(h, 1), span]
                 if masked:
                     scores = jnp.where(diagonal(), scores, NEG)
-                pull = nt(values, do_ref[h, span, :]) - st_ref[pl.ds(3 + h, 1), span]
-                grad = (jnp.exp2(scores) * pull).astype(BF16)
-                accum[h] += matmul(keys_t[h], grad)
-
-        lax.fori_loop(0, own, lambda b, _: (tile(b, False), 0)[1], 0)
-        tile(own, True)
+                pull = pull - st_ref[pl.ds(3 + h, 1), span]
+                grads.append((jnp.exp2(scores) * pull).astype(BF16))
+            for h in range(3):
+                accum[h] += matmul(keys_t[h], grads[h])
+
+        span_loop(0, own, 2, tile)
+        tile([own], True)
         for h in range(3):
-            dq_ref[slot, pl.ds(64 * h, 64), :] = accum[h] * 0.125
+            whole[pl.ds(64 * h, 64), :] = accum[h] * 0.125
+        dq_ref[span, :] = whole[...].T.astype(BF16)
 
 
 def key_kernel(g_ref, k_ref, v_ref, q_ref, do_ref, st_ref, dk_ref, dv_ref, acc_k, acc_v):
     g = g_ref[0]
+    parts = ((0, 128), (0, 128), (128, 64))
     for slot, own in ((0, g), (1, BLOCKS - 1 - g)):
         acc_k[...] = jnp.zeros_like(acc_k)
         acc_v[...] = jnp.zeros_like(acc_v)
         span = pl.ds(slot * HALF, HALF)
 
-        def tile(b, masked):
-            rows = pl.ds(block_row(b), HALF)
-            device = jnp.where(b < GROUPS, b, BLOCKS - 1 - b)
-            lanes = pl.ds(pl.multiple_of((b // GROUPS) * HALF, HALF), HALF)
-            stats = st_ref[device, :, lanes]
-            for h in range(3):
-                part, width = (pl.ds(0, 128), 128) if h < 2 else (pl.ds(128, 64), 64)
-                queries, grads = q_ref[rows, part], do_ref[rows, part]
-                keys, values = k_ref[h, span, :width], v_ref[h, span, :width]
-                scores = nt(keys, queries) * LOG2E - stats[h : h + 1]
+        def tile(blocks, masked):
+            rows = [pl.ds(block_row(b), HALF) for b in blocks]
+            stats = cat(
+                [
+                    st_ref[
+                        jnp.where(b < GROUPS, b, BLOCKS - 1 - b),
+                        :,
+                        pl.ds(pl.multiple_of((b // GROUPS) * HALF, HALF), HALF),
+                    ]
+                    for b in blocks
+                ],
+                1,
+            )
+            lanes = [pl.ds(at, width) for at, width in parts[1:]]
+            queries = [cat([q_ref[r, p] for r in rows]) for p in lanes]
+            grads = [cat([do_ref[r, p] for r in rows]) for p in lanes]
+            queries, grads = [queries[0]] + queries, [grads[0]] + grads
+            raw = [
+                (nt(k_ref[h, span, :width], queries[h]), nt(v_ref[h, span, :width], grads[h]))
+                for h, (_, width) in enumerate(parts)
+            ]
+            ready = []
+            for h, (scores, pull) in enumerate(raw):
+                scores = scores * LOG2E - stats[h : h + 1]
                 if masked:
                     scores = jnp.where(diagonal(), scores, NEG)
                 weights = jnp.exp2(scores)
-                pull = nt(values, grads) - stats[3 + h : 4 + h]
-                acc_v[h, :, :width] += matmul(weights.astype(BF16), grads)
-                acc_k[h, :, :width] += matmul((weights * pull).astype(BF16), queries)
-
-        tile(own, True)
-        lax.fori_loop(own + 1, BLOCKS, lambda b, _: (tile(b, False), 0)[1], 0)
+                pull = weights * (pull - stats[3 + h : 4 + h])
+                ready.append((weights.astype(BF16), pull.astype(BF16)))
+            for h, (weights, pull) in enumerate(ready):
+                width = parts[h][1]
+                acc_v[h, :, :width] += matmul(weights, grads[h])
+                acc_k[h, :, :width] += matmul(pull, queries[h])
+
+        tile([own], True)
+        span_loop(own + 1, BLOCKS, 4, tile)
         left = lax.broadcasted_iota(jnp.int32, (HALF, 128), 1) < 64
         for out, acc in ((dk_ref, acc_k), (dv_ref, acc_v)):
             out[span, pl.ds(0, 128)] = jnp.where(left, acc[0], acc[1]).astype(BF16)
@@ -227,6 +234,484 @@
 def natural_of(column):
     g, rest = column // 24, column % 24
     return 12 * (GROUPS * (rest // 12) + g) + rest % 12
+
+
+def team_peer(c, h, k):
+    return lax.rem(c + k // 2, 2), lax.rem(h + k % 2, 2)
+
+
+def greet(devices):
+    barrier = pltpu.get_barrier_semaphore()
+    for device in devices:
+        pl.semaphore_signal(barrier, inc=1, device_id=device, device_id_type=MESH)
+    pl.semaphore_wait(barrier, len(devices))
+
+
+def send(src, dst, sems, slot, device):
+    copy = pltpu.make_async_remote_copy(
+        src_ref=src,
+        dst_ref=dst,
+        send_sem=sems.at[0, slot],
+        recv_sem=sems.at[1, slot],
+        device_id=device,
+        device_id_type=MESH,
+    )
+    copy.start()
+    return copy
+
+
+def middle_kernel(
+    att_ref,
+    hid_ref,
+    cot_ref,
+    w_out_ref,
+    rows_ref,
+    w_fc_ref,
+    w_fc_t_ref,
+    w_proj_ref,
+    w_proj_t_ref,
+    vec_ref,
+    hidden_ref,
+    grad_mid_ref,
+    grad_attn_ref,
+    grad_pre_ref,
+    normed_ref,
+    activ_ref,
+    attended_ref,
+    grad_ref,
+    upper_ref,
+    norm_ref,
+    att,
+    mid,
+    grad_activ,
+    whole_out,
+    norm_out,
+    norm_in,
+    out_out,
+    out_in,
+    attn,
+    upper,
+    att_sems,
+    norm_sems,
+    out_sems,
+    attn_sems,
+    upper_sems,
+):
+    c, g, h = lax.axis_index("c"), lax.axis_index("g"), lax.axis_index("h")
+    rank = 2 * c + h
+    mirror = GROUPS - 1 - g
+    peers = [team_peer(c, h, k) for k in range(4)]
+    team = [(pc, g, ph) for pc, ph in peers[1:]]
+    across = [(pc, mirror, ph) for pc, ph in peers]
+    greet(team + across)
+
+    low, high = pl.ds(0, HALF), pl.ds(HALF, HALF)
+    copies = [
+        send(att_ref.at[low], att.at[rank, low], att_sems, k, device)
+        for k, device in enumerate(team)
+    ]
+    copies += [
+        send(att_ref.at[high], att.at[rank, high], att_sems, 3 + k, device)
+        for k, device in enumerate(across)
+    ]
+    att[rank, low, :] = att_ref[low, :]
+
+    cotangent = cot_ref[...]
+    thirds = [pl.ds(256 * k, 256) for k in range(3)]
+    for part in thirds:
+        grad_activ[:, part] = matmul(cotangent, w_proj_t_ref[:, part])
+    for copy in copies:
+        copy.wait_recv()
+
+    bias_out, gain, shift, bias_fc, bias_proj = (vec_ref[k : k + 1, :] for k in range(5))
+
+    total = hid_ref[...].astype(F32) + bias_out
+    for t in range(4):
+        total += matmul(att[t], w_out_ref[pl.ds(LOCAL * t, LOCAL), :])
+    mid[...] = total
+    normed_ref[...] = layer_norm(total, gain, shift).astype(BF16)
+    normed = normed_ref[...]
+    for part in thirds:
+        pre = matmul(normed, w_fc_ref[:, part]) + bias_fc[:, part.start : part.start + 256]
+        square = pre * pre
+        bend = jnp.tanh(GELU_ROOT * pre * (1.0 + GELU_CUBE * square))
+        activ_ref[:, part] = (0.5 * pre * (1.0 + bend)).astype(BF16)
+        slope = 0.5 * (1.0 + bend) + 0.5 * pre * (1.0 - bend * bend) * GELU_ROOT * (
+            1.0 + 3.0 * GELU_CUBE * square
+        )
+        grad_pre_ref[:, part] = (grad_activ[:, part] * slope).astype(BF16)
+
+    def spread_out(left, right_ref, whole, out, into, sems):
+        left = left[...]
+        for part in thirds:
+            whole[:, part] = matmul(left, right_ref[:, part])
+        copies = []
+        for k, (pc, ph) in enumerate(peers):
+            if k:
+                rows = pl.ds(pl.multiple_of(128 * (2 * pc + ph), 128), 128)
+                out[k] = whole[rows, :].astype(BF16)
+                copies.append(send(out.at[k], into.at[k], sems, k, team[k - 1]))
+        return copies
+
+    norm_copies = spread_out(grad_pre_ref, w_fc_t_ref, grad_activ, norm_out, norm_in, norm_sems)
+    out_copies = spread_out(activ_ref, w_proj_ref, whole_out, out_out, out_in, out_sems)
+    own = pl.ds(pl.multiple_of(128 * rank, 128), 128)
+    for copy in norm_copies:
+        copy.wait_recv()
+    grad_norm = grad_activ[own, :]
+    for k in (1, 2, 3):
+        grad_norm += norm_in[k].astype(F32)
+    own_mid = mid[own, :]
+    centred = own_mid - jnp.mean(own_mid, axis=-1, keepdims=True)
+    scale = lax.rsqrt(jnp.mean(centred * centred, axis=-1, keepdims=True) + EPS)
+    hat = centred * scale
+    pull = grad_norm * gain
+    pull = pull - jnp.mean(pull, axis=-1, keepdims=True)
+    pull = pull - hat * jnp.mean(pull * hat, axis=-1, keepdims=True)
+    grad_mid = cot_ref[own, :].astype(F32) + scale * pull
+    grad_mid_ref[...] = grad_mid
+    attn[rank] = grad_mid.astype(BF16)
+    attn_copies = [
+        send(attn.at[rank], attn.at[rank], attn_sems, k, device) for k, device in enumerate(team)
+    ]
+    norm_ref[...] = jnp.zeros_like(norm_ref)
+    norm_ref[0:1, :] = jnp.sum(grad_norm * hat, axis=0, keepdims=True)
+    norm_ref[1:2, :] = jnp.sum(grad_norm, axis=0, keepdims=True)
+    for copy in out_copies:
+        copy.wait_recv()
+    output = own_mid + bias_proj + whole_out[own, :]
+    for k in (1, 2, 3):
+        output += out_in[k].astype(F32)
+    hidden_ref[...] = output.astype(BF16)
+    for t in range(4):
+        attended_ref[t] = att[t]
+    for copy in attn_copies:
+        copy.wait_recv()
+    for t in (2, 3, 0, 1):
+        rows = pl.ds(128 * t, 128)
+        block = attn[t]
+        grad_attn_ref[rows, :] = block
+        grad_ref[rows, :] = trans_right(block, rows_ref[...]).astype(BF16)
+        if t == 3:
+            upper_copy = send(
+                grad_ref.at[high], upper, upper_sems, 0, (c, mirror, h)
+            )
+    upper_copy.wait_recv()
+    upper_ref[...] = upper[...]
+    for copy in copies + norm_copies + out_copies + attn_copies + [upper_copy]:
+        copy.wait_send()
+
+
+def middle(*args):
+    def out(shape, dtype):
+        return jax.ShapeDtypeStruct(shape, dtype)
+
+    vmem = pl.BlockSpec(memory_space=pltpu.VMEM)
+    outs = [
+        out((128, D), BF16),
+        out((128, D), F32),
+        out((512, D), BF16),
+        out((512, D), BF16),
+        out((512, D), BF16),
+        out((512, D), BF16),
+        out((4, 512, LOCAL), BF16),
+        out((512, LOCAL), BF16),
+        out((HALF, LOCAL), BF16),
+        out((8, D), F32),
+    ]
+    return pl.pallas_call(
+        middle_kernel,
+        out_shape=outs,
+        in_specs=[vmem] * len(args),
+        out_specs=[vmem] * len(outs),
+        scratch_shapes=[
+            pltpu.VMEM((4, 512, LOCAL), BF16),
+            pltpu.VMEM((512, D), F32),
+            pltpu.VMEM((512, D), F32),
+            pltpu.VMEM((512, D), F32),
+            pltpu.VMEM((4, 128, D), BF16),
+            pltpu.VMEM((4, 128, D), BF16),
+            pltpu.VMEM((4, 128, D), BF16),
+            pltpu.VMEM((4, 128, D), BF16),
+            pltpu.VMEM((4, 128, D), BF16),
+            pltpu.VMEM((HALF, LOCAL), BF16),
+            pltpu.SemaphoreType.DMA((2, 7)),
+            pltpu.SemaphoreType.DMA((2, 4)),
+            pltpu.SemaphoreType.DMA((2, 4)),
+            pltpu.SemaphoreType.DMA((2, 3)),
+            pltpu.SemaphoreType.DMA((2, 1)),
+        ],
+        compiler_params=pltpu.CompilerParams(
+            vmem_limit_bytes=VMEM_BYTES, collective_id=1, has_side_effects=True
+        ),
+        cost_estimate=pl.CostEstimate(
+            flops=9 * 512 * D * D, bytes_accessed=16 * 512 * D, transcendentals=512 * D
+        ),
+    )(*args)
+
+
+def wrap(value, size):
+    return lax.rem(value + size, size)
+
+
+class Plane:
+    def __init__(self, c, g, h):
+        self.c, self.g, self.h = c, g, h
+        self.y, self.z, self.core = g // 8, (g // 2) % 4, g % 2
+
+    def place(self, first, second, core):
+        dz = first * (1 - core) + second * core
+        dy = first * core + second * (1 - core)
+        return 8 * wrap(self.y + dy, 4) + 2 * wrap(self.z + dz, 4) + core
+
+    def device(self, first, second):
+        return (self.c, self.place(first, second, self.core), self.h)
+
+    def sibling(self):
+        return (self.c, self.g + 1 - 2 * self.core, self.h)
+
+
+def shift_of(index):
+    return ((index + 1) % 3 + 1) * jnp.minimum(index, 1)
+
+
+def travel(plane, held, near_sems, pair_sems):
+    def halves():
+        return (pl.ds(0, HALF), pl.ds(HALF, HALF))
+
+    def source(d, e, core):
+        return plane.place(shift_of(d), shift_of(e), core)
+
+    def copy(n, half, slot, first, second):
+        rows = halves()[half]
+        return pltpu.make_async_remote_copy(
+            src_ref=held.at[slot, rows],
+            dst_ref=held.at[slot, rows],
+            send_sem=near_sems.at[0, half, n],
+            recv_sem=near_sems.at[1, half, n],
+            device_id=plane.device(first, second),
+            device_id_type=MESH,
+        )
+
+    def across(n, slot):
+        return pltpu.make_async_remote_copy(
+            src_ref=held.at[slot],
+            dst_ref=held.at[slot],
+            send_sem=pair_sems.at[0, n],
+            recv_sem=pair_sems.at[1, n],
+            device_id=plane.sibling(),
+            device_id_type=MESH,
+        )
+
+    def each(n, act):
+        d, e = n % 4, n // 4
+        slot = source(d, e, plane.core)
+        act(across(n, slot))
+
+        @pl.when(n == 0)
+        def _():
+            for half in (0, 1):
+                act(copy(1, half, slot, 1, 0))
+                act(copy(2, half, slot, 3, 0))
+
+        @pl.when(n == 1)
+        def _():
+            act(copy(3, 0, slot, 1, 0))
+
+        @pl.when(n == 2)
+        def _():
+            act(copy(3, 1, slot, 3, 0))
+
+        @pl.when(e == 0)
+        def _():
+            for half in (0, 1):
+                act(copy(4 + d, half, slot, 0, 1))
+                act(copy(8 + d, half, slot, 0, 3))
+
+        @pl.when(e == 1)
+        def _():
+            act(copy(12 + d, 0, slot, 0, 1))
+
+        @pl.when(e == 2)
+        def _():
+            act(copy(12 + d, 1, slot, 0, 3))
+
+    def depart(n):
+        each(n, lambda c: c.start())
+
+    def arrive(n):
+        for half in (0, 1):
+            copy(n, half, source(n % 4, n // 4, plane.core), 0, 1).wait_recv()
+        depart(n)
+
+    def arrive_across(n):
+        across(n, source(n % 4, n // 4, 1 - plane.core)).wait_recv()
+
+    def finish():
+        def sent(n, carry):
+            each(n, lambda c: c.wait_send())
+            return carry
+
+        lax.fori_loop(0, 16, sent, 0)
+
+    def place_of(n, other):
+        return source(n % 4, n // 4, plane.core + other - 2 * plane.core * other)
+
+    return depart, arrive, arrive_across, place_of, finish
+
+
+def fused_forward_kernel(
+    q_ref, kv_ref, att_ref, nat_ref, lse_ref, all_ref, held, qz, upper, top, total, accum,
+    near_sems, pair_sems, upper_sems, out_sems,
+):
+    c, g, h = lax.axis_index("c"), lax.axis_index("g"), lax.axis_index("h")
+    plane = Plane(c, g, h)
+    mirror = (c, GROUPS - 1 - g, h)
+    greet(
+        [plane.sibling(), plane.device(1, 0), plane.device(3, 0)]
+        + [plane.device(0, 1), plane.device(0, 3), mirror]
+    )
+    swap = send(q_ref.at[pl.ds(HALF, HALF)], upper, upper_sems, 0, mirror)
+    held[g] = kv_ref[...]
+    depart, arrive, arrive_across, place_of, finish = travel(plane, held, near_sems, pair_sems)
+    top[...] = jnp.full_like(top, NEG)
+    total[...] = jnp.zeros_like(total)
+    accum[...] = jnp.zeros_like(accum)
+    left = lax.broadcasted_iota(jnp.int32, (HALF, 128), 1) < 64
+
+    def place_queries(slot, block):
+        span = pl.ds(slot * HALF, HALF)
+        pair = block[:, :128].astype(F32)
+        qz[0, span, :] = jnp.where(left, pair, 0.0).astype(BF16)
+        qz[1, span, :] = jnp.where(left, 0.0, pair).astype(BF16)
+        qz[2, span, :] = jnp.concatenate(
+            [block[:, 128:], jnp.zeros((HALF, 64), BF16)], axis=1
+        )
+
+    place_queries(0, q_ref[pl.ds(0, HALF), :])
+
+    def tiles(device, units):
+        chains = []
+        for slot, halves, masked in units:
+            rows = pl.ds(halves[0] * HALF, len(halves) * HALF)
+            span = pl.ds(slot * HALF, HALF)
+            first, second, third = (held[device, rows, pl.ds(128 * k, 128)] for k in range(3))
+            second_t, third_t = second.T, third.T
+            values = (second_t[64:], third_t[:64], third_t[64:])
+            for n, keys in enumerate((first, first, second)):
+                scores = nt(keys, qz[n, span, :])
+                if masked:
+                    scores = jnp.where(diagonal(), scores, NEG)
+                chains.append((slot, n, values[n], scores))
+        ready = []
+        for slot, n, value, scores in chains:
+            line = pl.ds(8 * slot + n, 1)
+            old = top[line, :]
+            new = jnp.maximum(old, jnp.max(scores, axis=0, keepdims=True))
+            weights = jnp.exp(scores - new)
+            fade = jnp.exp(old - new)
+            top[line, :] = new
+            total[line, :] = total[line, :] * fade + jnp.sum(weights, axis=0, keepdims=True)
+            ready.append((slot, n, value, weights.astype(BF16), fade))
+        for slot, n, value, weights, fade in ready:
+            accum[slot, n] = accum[slot, n] * fade + matmul(value, weights)
+
+    def keep(slot):
+        return pltpu.make_async_copy(held.at[slot], all_ref.at[slot], out_sems.at[slot])
+
+    def work(device):
+        keep(device).start()
+
+        low, high = device < g, device < GROUPS - 1 - g
+
+        @pl.when(low & high)
+        def _():
+            tiles(device, [(0, (0,), False), (1, (0, 1), False)])
+
+        @pl.when(low & ~high)
+        def _():
+            tiles(device, [(0, (0,), False), (1, (0,), False)])
+
+        @pl.when(~low & high)
+        def _():
+            tiles(device, [(1, (0, 1), False)])
+
+        @pl.when(~low & ~high)
+        def _():
+            tiles(device, [(1, (0,), False)])
+
+        @pl.when(device == g)
+        def _():
+            tiles(device, [(0, (0,), True)])
+
+        @pl.when(device == GROUPS - 1 - g)
+        def _():
+            tiles(device, [(1, (1,), True)])
+
+    lax.fori_loop(0, 1, lambda n, carry: (depart(n), carry)[1], 0)
+    swap.wait_recv()
+    place_queries(1, upper[...])
+
+    def step(m, carry):
+        n, other = m // 2, m % 2
+
+        @pl.when((other == 0) & (n > 0))
+        def _():
+            arrive(n)
+
+        @pl.when(other == 1)
+        def _():
+            arrive_across(n)
+
+        work(place_of(n, other))
+        return carry
+
+    lax.fori_loop(0, 32, step, 0)
+    for slot in range(2):
+        for n in range(3):
+            line = pl.ds(8 * slot + n, 1)
+            att_ref[slot, pl.ds(64 * n, 64), :] = accum[slot, n] / total[line, :]
+        span = pl.ds(slot * HALF, HALF)
+        nat_ref[span, :] = att_ref[slot].T.astype(BF16)
+        lines = pl.ds(8 * slot, 8)
+        lse_ref[:, span] = (top[lines, :] + jnp.log(jnp.maximum(total[lines, :], 1e-30))) * LOG2E
+    swap.wait_send()
+    finish()
+    for slot in range(GROUPS):
+        keep(slot).wait()
+
+
+def fused_forward(queries, kv):
+    vmem = pl.BlockSpec(memory_space=pltpu.VMEM)
+    return pl.pallas_call(
+        fused_forward_kernel,
+        out_shape=[
+            jax.ShapeDtypeStruct((2, LOCAL, HALF), F32),
+            jax.ShapeDtypeStruct((512, LOCAL), BF16),
+            jax.ShapeDtypeStruct((8, 512), F32),
+            jax.ShapeDtypeStruct((GROUPS, 512, 2 * LOCAL), BF16),
+        ],
+        in_specs=[vmem, vmem],
+        out_specs=[vmem, vmem, vmem, pl.BlockSpec(memory_space=pl.ANY)],
+        scratch_shapes=[
+            pltpu.VMEM((GROUPS, 512, 2 * LOCAL), BF16),
+            pltpu.VMEM((3, 512, 128), BF16),
+            pltpu.VMEM((HALF, LOCAL), BF16),
+            pltpu.VMEM((16, HALF), F32),
+            pltpu.VMEM((16, HALF), F32),
+            pltpu.VMEM((2, 3, 64, HALF), F32),
+            pltpu.SemaphoreType.DMA((2, 2, 16)),
+            pltpu.SemaphoreType.DMA((2, 16)),
+            pltpu.SemaphoreType.DMA((2, 1)),
+            pltpu.SemaphoreType.DMA((GROUPS,)),
+        ],
+        compiler_params=pltpu.CompilerParams(
+            vmem_limit_bytes=VMEM_BYTES, collective_id=2, has_side_effects=True
+        ),
+        cost_estimate=pl.CostEstimate(
+            flops=65 * 3 * HALF * HALF * 1024, bytes_accessed=32 << 20, transcendentals=65 * 3 * HALF * HALF
+        ),
+    )(queries, kv)
 
 
 def on_device(
@@ -249,8 +734,9 @@
     rank = 2 * c + h
     where_am_i = g.astype(jnp.int32)[None]
 
-    tokens = jnp.concatenate(team_gather(jnp.concatenate([hidden_in, out_grad], axis=1)), axis=0)
-    resid, cotangent = tokens[:, :D].astype(F32), tokens[:, D:]
+    tokens = jnp.concatenate(team_gather(hidden_in), axis=0)
+    resid = tokens.astype(F32)
+    cotangent = jnp.concatenate(team_gather(out_grad), axis=0)
 
     reorder = one_hot(D, D, natural_of)
     pick_units = one_hot(1536, D, lambda k: 48 * (k // 24) + 24 * h + k % 24)
@@ -304,61 +790,53 @@
     normed1 = layer_norm(resid, gain_one, shift_one).astype(BF16)
     qkv = (matmul(normed1, w_qkv_t) + bias_here).astype(BF16)
     queries = qkv[:, :LOCAL] * jnp.asarray(0.125, BF16)
-    kv_all = lax.all_gather(qkv[:, LOCAL:], "g", axis=0, tiled=True)
     query_all = lax.all_gather(queries, "g", axis=0, tiled=True)
+    att_t, attended_zz, lse, kv_all = fused_forward(queries, qkv[:, LOCAL:])
+    kv_all = kv_all.reshape(TOKENS, 2 * LOCAL)
     query_zz = sides(swap_upper(queries), (False, True, False))
-    att_t, lse = attention_call(
-        forward_kernel,
-        [
-            jax.ShapeDtypeStruct((2, LOCAL, HALF), F32),
-            jax.ShapeDtypeStruct((8, 512), F32),
-        ],
-        [
-            pltpu.VMEM((8, HALF), F32),
-            pltpu.VMEM((8, HALF), F32),
-            pltpu.VMEM((3, 64, HALF), F32),
-        ],
-        2,
-        where_am_i,
-        query_zz,
-        kv_all,
-    )
-    attended = att_t.transpose(0, 2, 1).reshape(512, LOCAL).astype(BF16)
-    attended = jnp.concatenate(team_gather(swap_upper(attended)), axis=1)
-
-    mid = resid + matmul(attended, w_out_all) + bias_out
-    normed2 = layer_norm(mid, gain_two, shift_two).astype(BF16)
-    pre_fc = matmul(normed2, w_fc_t) + bias_fc
-    activ = gelu_tanh(pre_fc).astype(BF16)
-    grad_activ = trans_right(cotangent, w_proj_t)
-    grad_pre = jax.vjp(gelu_tanh, pre_fc)[1](grad_activ)[0].astype(BF16)
-    grad_norm2 = team_scatter_sum(trans_right(grad_pre, w_fc_t))
-    own_rows = lambda v: lax.dynamic_slice_in_dim(v, 128 * rank, 128, 0)
-    mid_own = own_rows(mid)
-    grad_mid_ln, grad_gain2, grad_shift2 = jax.vjp(layer_norm, mid_own, gain_two, shift_two)[1](
-        grad_norm2
-    )
+    w_out_rows = lax.dynamic_slice_in_dim(w_out_all, LOCAL * rank, LOCAL, 0)
+    vec = jnp.stack([bias_out, gain_two, shift_two, bias_fc, bias_proj])
+    (
+        hidden_out,
+        grad_mid,
+        grad_attn_all,
+        grad_pre,
+        normed2,
+        activ,
+        attended,
+        grad_heads,
+        grad_upper,
+        norm_sums,
+    ) = middle(
+        attended_zz,
+        tokens,
+        cotangent,
+        w_out_all,
+        w_out_rows,
+        w_fc_t,
+        w_fc_t.T,
+        w_proj_t,
+        w_proj_t.T,
+        jnp.concatenate([vec, jnp.zeros((3, D), F32)], axis=0),
+    )
+    attended = jnp.concatenate([attended[t] for t in range(4)], axis=1)
+    grad_gain2, grad_shift2 = norm_sums[0], norm_sums[1]
+    grad_attn = lax.dynamic_slice_in_dim(grad_attn_all, 128 * rank, 128, 0)
     grad_output = out_grad.astype(F32)
-    grad_mid = grad_output + grad_mid_ln
-    grad_attn = grad_mid.astype(BF16)
-    grad_attn_all = jnp.concatenate(team_gather(grad_attn), axis=0)
-    w_out_rows = lax.dynamic_slice_in_dim(w_out_all, LOCAL * rank, LOCAL, 0)
-    grad_heads = trans_right(grad_attn_all, w_out_rows).astype(BF16)
     grad_heads_all = lax.all_gather(grad_heads, "g", axis=0, tiled=True)
-    grad_zz = swap_upper(grad_heads)
+    grad_zz = jnp.concatenate([grad_heads[:HALF], grad_upper], axis=0)
     grad_zz_t = grad_zz.reshape(2, HALF, LOCAL).transpose(0, 2, 1)
     delta = jnp.sum((grad_zz_t.astype(F32) * att_t).reshape(2, 3, 64, HALF), axis=2)
     delta = delta.transpose(1, 0, 2).reshape(3, 512)
     stats = jnp.concatenate([lse[:3], delta, jnp.zeros((2, 512), F32)], axis=0)
-    stats_all = lax.all_gather(stats, "g", axis=0, tiled=False)
-
-    output = mid_own + bias_proj + team_scatter_sum(matmul(activ, w_proj_t))
-    hidden_out = output.astype(BF16)
-
-    (dq_t,) = attention_call(
+    stats_all = lax.all_to_all(
+        jnp.broadcast_to(stats[None], (GROUPS, 8, 512)), "g", 0, 0, tiled=True
+    )
+
+    (dq,) = attention_call(
         query_kernel,
-        [jax.ShapeDtypeStruct((2, LOCAL, HALF), F32)],
-        [pltpu.VMEM((3, 64, HALF), F32)],
+        [jax.ShapeDtypeStruct((512, LOCAL), BF16)],
+        [pltpu.VMEM((3, 64, HALF), F32), pltpu.VMEM((LOCAL, HALF), F32)],
         3,
         where_am_i,
         query_zz,
@@ -382,7 +860,7 @@
         grad_heads_all,
         stats_all,
     )
-    grad_q = swap_upper(dq_t.transpose(0, 2, 1).reshape(512, LOCAL).astype(BF16))
+    grad_q = swap_upper(dq)
     grad_kv = swap_upper(jnp.concatenate([dk, dv], axis=1))
     grad_qkv = jnp.concatenate([grad_q, grad_kv], axis=1)
     grad_norm1 = team_scatter_sum(trans_right(grad_qkv, w_qkv_t))

time: 553 us -> 458 us (0.83)
  waiting for transfers between devices: 155 us -> 87 us
  blocking collectives: 23.1 us -> 0 us
  Pallas kernels: 183 us -> 198 us
  starting transfers between devices: 63.2 us -> 49 us
  local copies, waits for them, and re-layouts: 45.1 us -> 56.5 us
  matrix products: 30.2 us -> 23.2 us
  other arithmetic: 28.2 us -> 22.6 us
    pallas_call x0 -> x2, Pallas kernels: none -> 131 us  [the longest x1 66.4 us: fused_forward(): pl.pallas_call(fused_forward_kernel, out_shape=[jax.ShapeDtypeStruct((2,...]
    pallas_call x3 -> x2, Pallas kernels: 183 us -> 67.4 us  [attention_call(): pl.pallas_call(kernel, out_shape=outs, in_specs=[pl.BlockSpec(memory_spac...]
    all_gather x1 -> x0, waiting for transfers between devices: 46 us -> none  [on_device(): kv_all = lax.all_gather(qkv[:, LOCAL:], 'g', axis=0, tiled=True)]
    all_gather x1 -> x0, blocking collectives: 23.1 us -> none  [on_device(): stats_all = lax.all_gather(stats, 'g', axis=0, tiled=False)]
    ppermute x7 -> x4, waiting for transfers between devices: 30.6 us -> 18.8 us  [team_others(): lax.ppermute(parts[1], 'c', SWAP)]
    ppermute x5 -> x3, starting transfers between devices: 17.8 us -> 7.88 us  [swap_upper(): lax.ppermute(value[HALF:], 'g', MIRROR)]
    slice x2 -> x3, local copies, waits for them, and re-layouts: 0.01 us -> 7.32 us  [on_device(): w_fc_t, w_out_all, w_proj_t = (rest[:, :D], rest[:, D:], second[:, 2 * D:])]
    ppermute x7 -> x4, starting transfers between devices: 16.4 us -> 9.88 us  [team_others(): lax.ppermute(parts[1], 'c', SWAP)]
  transfers between devices with their start and end apart: 35 -> 24, of which waited for: 22 -> 16; matrix products, arithmetic and copies ran while one was open for 14% -> 18% of each run, Pallas kernels for 34% -> 44%
where the time goes in v2:
time: 458 us; the launch traced here: 452 us
  Pallas kernels  198 us (43%)
  waiting for transfers between devices  87 us (19%)
  local copies, waits for them, and re-layouts  56.5 us (12%)
  starting transfers between devices  49 us (11%)
  matrix products  23.2 us (5%)
  other arithmetic  22.6 us (5%)
  between operations  15.4 us (3%)
    pallas_call x2, Pallas kernels, attention_call(): pl.pallas_call(kernel, out_shape=outs, in_specs=[pl.BlockSpec(memory_spac...  67.4 us
    pallas_call x1, Pallas kernels, fused_forward(): pl.pallas_call(fused_forward_kernel, out_shape=[jax.ShapeDtypeStruct((2,...  66.4 us
    pallas_call x1, Pallas kernels, middle(): pl.pallas_call(middle_kernel, out_shape=outs, in_specs=[vmem] * len(args)...  64.3 us
    all_gather x1, waiting for transfers between devices, on_device(): first = lax.all_gather(both(mine[0], theirs[0]), 'g', axis=0, tiled=True)  27.9 us
    ppermute x4, waiting for transfers between devices, team_others(): lax.ppermute(parts[1], 'c', SWAP)  18.8 us
    all_to_all x2, starting transfers between devices, sum_over_g(): lines = lax.all_to_all(lines, 'g', 0, 0, tiled=True)  14.1 us
    all_to_all x2, waiting for transfers between devices, sum_over_g(): lines = lax.all_to_all(lines, 'g', 0, 0, tiled=True)  13.9 us
    dot_general x4, matrix products, trans_left(): lax.dot_general(left, right, (((0,), (0,)), ((), ())), preferred_element_...  12.3 us
  transfers between devices with their start and end apart: 24, of which 16 were waited for; matrix products, arithmetic and copies ran while one was open for 18% of the time, Pallas kernels for 44%

profile of v2, /device:TPU:1, one launch (start us, length us, event | category | flops | bytes accessed | tf_op | source)
XLA Modules:
  0.0 451.8 jit_solution(9196442365498237994)
XLA Ops:
  7.3 5.4 %concatenate.137 = bf16[144]{0:T(256)(128)(2,1)S(1)} concatenate(bf16[12]{0:T(256)(128)(2,1)} %param.15, bf16[12]{0:T(256)(128)(2,1)} %param.16, bf16[24]{0:T(256)(128)(2,1)} %param.18, bf16[12]{0:T(256)(128)(2,1)} %param.20, bf16[12]{0:T(256)(128)(2,1)} %param.21, bf16[12]{0:T(256)(128)(2,1)} %param.22, bf16[48]{0:T(256)(128)(2,1)} %param.24, bf16[12]{0:T(256)(128)(2,1)} %param.26), dimensions={0} | concatenate | bytes 576 | tf_op jit(solution)/shard_map/concatenate | solution.py:743
  13.8 3.6 collective-permute-start.3
  21.3 3.0 collective-permute-start.7
  28.1 2.4 collective-permute-start.1
  31.2 5.2 %collective-permute-done.1 = bf16[128,768]{1,0:T(8,128)(2,1)S(1)} collective-permute-done((bf16[128,768]{1,0:T(8,128)(2,1)S(1)}, bf16[128,768]{1,0:T(8,128)(2,1)S(1)}, u32[]{:S(2)}, u32[]{:S(2)}) %collective-permute-start.1) | collective-permute-done | bytes 196640 | tf_op jit(solution)/shard_map/ppermute | solution.py:57
  36.4 1.8 collective-permute-done.2
  38.9 27.9 %all-gather.5.cloned.1.call-done = bf16[768,704]{1,0:T(8,128)(2,1)} async-done(((bf16[24,704]{1,0:T(8,128)(2,1)}), bf16[768,704]{1,0:T(8,128)(2,1)}) %all-gather.5.cloned.1.call-update) | async-done | bytes 1081360 | tf_op jit(solution)/shard_map/all_gather | solution.py:764
  68.9 2.2 convolution_convert_fusion.4
  74.1 2.4 collective-permute-start.5
  77.2 2.0 collective-permute-done.4
  79.2 6.4 %collective-permute-done.5 = bf16[128,768]{1,0:T(8,128)(2,1)S(1)} collective-permute-done((bf16[128,768]{1,0:T(8,128)(2,1)S(1)}, bf16[128,768]{1,0:T(8,128)(2,1)S(1)}, u32[]{:S(2)}, u32[]{:S(2)}) %collective-permute-start.5) | collective-permute-done | bytes 196640 | tf_op jit(solution)/shard_map/ppermute | solution.py:57
  85.6 2.9 collective-permute-done.6
  92.5 66.4 %shard_map.245 = (f32[2,192,256]{2,1,0:T(8,128)S(1)}, bf16[512,192]{1,0:T(8,128)(2,1)S(1)}, f32[8,512]{1,0:T(8,128)S(1)}, bf16[32,512,384]{2,1,0:T(8,128)(2,1)}) custom-call(bf16[512,192]{1,0:T(8,128)(2,1)S(1)} %copy-done.2, bf16[512,384]{1,0:T(8,128)(2,1)S(1)} %slice.371.kv_ref), custom_call_target="tpu_custom_call" | custom-call | flops 13086228480 | bytes 33554432 | tf_op jit(solution)/shard_map/pallas_call | solution.py:686
  158.9 4.7 %convolution_convert_fusion = bf16[768,1536]{0,1:T(8,128)(2,1)S(1)} fusion(bf16[768,2304]{1,0:T(8,128)(2,1)} %all-gather.7.cloned.1.call-done, s32[768]{0:T(1024)S(1)} %get-tuple-element.150, s32[768]{0:T(1024)S(1)} %get-tuple-element.153, s32[768]{0:T(1024)S(1)} %get-tuple-element.151, s32[768]{0:T(1024)S(1)} %get-tuple-element.152, ...), kind=kOutput, calls=%fused_computation.10 | convolution fusion | flops 1824325632 | bytes 4732416 | tf_op jit(solution)/shard_map/dot_general | solution.py:32
  163.6 2.0 slice_bitcast_fusion.14
  165.6 2.4 copy.82.w_out_ref
  168.0 2.4 copy.84.w_fc_ref
  171.8 2.5 slice.375.w_proj_ref
  174.3 2.5 copy.101
  176.9 64.3 %shard_map.246 = (bf16[128,768]{1,0:T(8,128)(2,1)S(1)}, f32[128,768]{1,0:T(8,128)S(1)}, bf16[512,768]{1,0:T(8,128)(2,1)S(1)}, bf16[512,768]{1,0:T(8,128)(2,1)S(1...) custom-call(bf16[512,192]{1,0:T(8,128)(2,1)S(1)} %get-tuple-element., ...), custom_call_target="tpu_custom_call" | custom-call | flops 2717908992 | bytes 6291456 | tf_op jit(solution)/shard_map/pallas_call | solution.py:422
  246.1 2.3 collective-permute-start.8
  249.9 4.9 %collective-permute-done.8 = bf16[256,192]{1,0:T(8,128)(2,1)S(1)} collective-permute-done((bf16[256,192]{1,0:T(8,128)(2,1)S(1)}, bf16[256,192]{1,0:T(8,128)(2,1)S(1)}, u32[]{:S(2)}, u32[]{:S(2)}) %collective-permute-start.8) | collective-permute-done | bytes 98336 | tf_op jit(solution)/shard_map/ppermute | solution.py:214
  258.4 1.9 copy.86
  260.3 1.8 bitcast_multiply_fusion
  264.1 4.0 all-to-all-start
  268.1 2.2 slice_bitcast_fusion.3
  270.3 3.4 fusion.30
  273.7 1.9 copy.96
  276.8 3.9 convolution_convert_fusion.2
  282.8 30.5 %shard_map.247 = bf16[512,192]{1,0:T(8,128)(2,1)S(1)} custom-call(s32[1]{0:T(128)} %bitcast.3.g_ref, bf16[3,512,128]{2,1,0:T(8,128)(2,1)S(1)} %copy-done.3, bf16[3,512,128]{2,1,0:T(8,128)(2,1)S(1)} %copy-done.4, f32[8,512]{1,0:T(8,128)S(1)} %maximum_maximum_fusion.1.st_ref, bf16[16384,384]{1,0:T(8,128)(2,1)} %bitcast.109), custom_call_target="tpu_custom_call" | custom-call | flops 19629342720 | bytes 13385732 | tf_op jit(solution)/shard_map/pallas_call | solution.py:196
  313.4 1.8 convolution_convert_fusion.1
  315.2 5.7 %concatenate.177 = bf16[32,24,1728]{2,1,0:T(8,128)(2,1)} concatenate(bf16[32,24,768]{2,1,0:T(8,128)(2,1)} %bitcast.100, bf16[32,24,192]{2,1,0:T(8,128)(2,1)} %bitcast.98, bf16[32,24,768]{2,1,0:T(8,128)(2,1)} %bitcast.101), dimensions={2} | concatenate | bytes 5308416 | tf_op jit(solution)/shard_map/concatenate | solution.py:887
  321.6 7.4 %all-to-all-start.2 = ((bf16[32,24,1728]{2,1,0:T(8,128)(2,1)}), bf16[32,24,1728]{2,1,0:T(8,128)(2,1)}, u32[]{:S(2)}, u32[]{:S(2)}) async-start(bf16[32,24,1728]{2,1,0:T(8,128)(2,1)} %concatenate.177), calls=%async_computation.2 | async-start | bytes 5505024 | tf_op jit(solution)/shard_map/all_to_all | solution.py:884
  329.1 36.9 %shard_map.248 = (bf16[512,192]{1,0:T(8,128)(2,1)S(1)}, bf16[512,192]{1,0:T(8,128)(2,1)S(1)}) custom-call(s32[1]{0:T(128)} %bitcast.3.g_ref, bf16[3,512,128]{2,1,0:T(8,128)(2,1)S(1)} %pad_maximum_fusion.5.k_ref, bf16[3,512,128]{2,1,0:T(8,128)(2,1)S(1)} %pad_maximum_fusion.6.v_ref, bf16[16384,192]{1,0:T(8,128)(2,1)} %all-gather.9.cloned.1.call-done.q_ref, ...), custom_call_target="tpu_custom_call" | custom-call | flops 26172456960 | bytes 13893636 | tf_op jit(solution)/shard_map/pallas_call | solution.py:196
  366.1 5.3 %collective-permute-start.10 = (bf16[256,384]{1,0:T(8,128)(2,1)S(1)}, bf16[256,384]{1,0:T(8,128)(2,1)S(1)}, u32[]{:S(2)}, u32[]{:S(2)}) collective-permute-start(bf16[256,384]{1,0:T(8,128)(2,1)S(1)} %get-tuple-element.77), channel_id=1, source_target_pairs={{0,62},{2,60},{4,58},{6,56},{8,54},{10,52},{12,50},{14,48},{16,46}... | collective-permute-start | bytes 589832 | tf_op jit(solution)/shard_map/ppermute | solution.py:214
  374.1 6.6 %collective-permute-done.9 = bf16[256,192]{1,0:T(8,128)(2,1)S(1)} collective-permute-done((bf16[256,192]{1,0:T(8,128)(2,1)}, bf16[256,192]{1,0:T(8,128)(2,1)S(1)}, u32[]{:S(2)}, u32[]{:S(2)}) %collective-permute-start.9) | collective-permute-done | bytes 98336 | tf_op jit(solution)/shard_map/ppermute | solution.py:214
  380.7 2.1 fusion.104
  383.8 2.4 collective-permute-start.12
  387.9 3.1 convolution_convert_fusion.3
  391.9 3.7 collective-permute-done.12
  395.6 2.2 collective-permute-done.13
  401.6 6.7 %all-to-all-start.1 = ((bf16[32,24,640]{2,1,0:T(8,128)(2,1)}), bf16[32,24,640]{2,1,0:T(8,128)(2,1)S(1)}, u32[]{:S(2)}, u32[]{:S(2)}) async-start(bf16[32,24,640]{2,1,0:T(8,128)(2,1)} %pad_maximum_fusion), calls=%async_computation.1 | async-start | bytes 1966080 | tf_op jit(solution)/shard_map/all_to_all | solution.py:884
  408.3 2.2 reduce.3
  410.5 13.9 %all-to-all-done.1 = bf16[32,24,640]{2,1,0:T(8,128)(2,1)S(1)} async-done(((bf16[32,24,640]{2,1,0:T(8,128)(2,1)}), bf16[32,24,640]{2,1,0:T(8,128)(2,1)S(1)}, u32[]{:S(2)}, u32[]{:S(2)}) %all-to-all-start.1) | async-done | bytes 983072 | tf_op jit(solution)/shard_map/all_to_all | solution.py:884
  424.7 2.6 collective-permute-start.15
  429.5 3.5 collective-permute-done.15
  433.0 2.5 collective-permute-done.16
  438.9 1.8 reshape.164
  (268 shorter events, 56.4 us)
Async XLA Ops:
  7.2 17.2 %copy-start = (bf16[48,768]{1,0:T(8,128)(2,1)S(1)}, bf16[48,768]{1,0:T(8,128)(2,1)}, u32[]{:S(2)}) copy-start(bf16[48,768]{1,0:T(8,128)(2,1)} %param.25) | copy-start | bytes 221188
  7.2 59.6 %all-gather.5.cloned.1.call-start = ((), (), s32[]{:S(2)}) async-start(), calls=%async_computation.3 | async-start | bytes 1216512 | tf_op jit(solution)/shard_map/all_gather | solution.py:764
  13.8 4.8 %collective-permute-start.3 = (bf16[12,704]{1,0:T(8,128)(2,1)S(1)}, bf16[12,704]{1,0:T(8,128)(2,1)S(1)}, u32[]{:S(2)}, u32[]{:S(2)}) collective-permute-start(bf16[12,704]{1,0:T(8,128)(2,1)S(1)} %fusion.87), channel_id=1, source_target_pairs={{0,64},{64,0},{1,65},{65,1},{2,66},{66,2},{3,67},{67,3},{4,68},{68... | collective-permute-start | bytes 50696 | tf_op jit(solution)/shard_map/ppermute | solution.py:759
  17.4 259.4 %copy-start.30 = (s32[768]{0:T(1024)}, s32[768]{0:T(1024)S(1)}, u32[]{:S(2)}) copy-start(s32[768]{0:T(1024)S(1)} %get-tuple-element.150) | copy-start | bytes 9220
  17.4 259.4 %copy-start.32 = (s32[768]{0:T(1024)}, s32[768]{0:T(1024)S(1)}, u32[]{:S(2)}) copy-start(s32[768]{0:T(1024)S(1)} %get-tuple-element.151) | copy-start | bytes 9220
  17.4 259.4 %copy-start.34 = (s32[768]{0:T(1024)}, s32[768]{0:T(1024)S(1)}, u32[]{:S(2)}) copy-start(s32[768]{0:T(1024)S(1)} %get-tuple-element.152) | copy-start | bytes 9220
  17.4 259.4 %copy-start.36 = (s32[768]{0:T(1024)}, s32[768]{0:T(1024)S(1)}, u32[]{:S(2)}) copy-start(s32[768]{0:T(1024)S(1)} %get-tuple-element.153) | copy-start | bytes 9220
  19.3 139.5 %all-gather.7.cloned.1.call-start = ((), (), s32[]{:S(2)}) async-start(), calls=%async_computation.4 | async-start | bytes 3649536 | tf_op jit(solution)/shard_map/all_gather | solution.py:766
  19.4 139.5 %copy-start.39 = (pred[768]{0:T(1024)(128)(4,1)}, pred[768]{0:T(1024)(128)(4,1)S(1)}, u32[]{:S(2)}) copy-start(pred[768]{0:T(1024)(128)(4,1)S(1)} %get-tuple-element.148) | copy-start | bytes 2308
  19.4 139.5 %copy-start.41 = (pred[768]{0:T(1024)(128)(4,1)}, pred[768]{0:T(1024)(128)(4,1)S(1)}, u32[]{:S(2)}) copy-start(pred[768]{0:T(1024)(128)(4,1)S(1)} %get-tuple-element.149) | copy-start | bytes 2308
  21.3 4.5 %collective-permute-start.7 = (bf16[12,1536]{1,0:T(8,128)(2,1)S(1)}, bf16[12,1536]{1,0:T(8,128)(2,1)S(1)}, u32[]{:S(2)}, u32[]{:S(2)}) collective-permute-start(bf16[12,1536]{1,0:T(8,128)(2,1)S(1)} %pad_maximum_fusion.12), channel_id=1, source_target_pairs={{0,64},{64,0},{1,65},{65,1},{2,66},{66,2},{3,67},{67,3},{4,68},{68... | collective-permute-start | bytes 110600 | tf_op jit(solution)/shard_map/ppermute | solution.py:759
  26.5 302.5 %all-gather.9.cloned.1.call-start = ((), (), s32[]{:S(2)}) async-start(), calls=%async_computation.5 | async-start | bytes 8650752 | tf_op jit(solution)/shard_map/all_gather | solution.py:793
  26.6 4.6 %collective-permute-start = (bf16[128,768]{1,0:T(8,128)(2,1)S(1)}, bf16[128,768]{1,0:T(8,128)(2,1)S(1)}, u32[]{:S(2)}, u32[]{:S(2)}) collective-permute-start(bf16[128,768]{1,0:T(8,128)(2,1)S(1)} %copy-done.11), channel_id=1, source_target_pairs={{0,1},{1,0},{2,3},{3,2},{4,5},{5,4},{6,7},{7,6},{8,9},{9,8},{10,11... | collective-permute-start | bytes 589832 | tf_op jit(solution)/shard_map/ppermute | solution.py:56
  28.1 8.3 %collective-permute-start.1 = (bf16[128,768]{1,0:T(8,128)(2,1)S(1)}, bf16[128,768]{1,0:T(8,128)(2,1)S(1)}, u32[]{:S(2)}, u32[]{:S(2)}) collective-permute-start(bf16[128,768]{1,0:T(8,128)(2,1)S(1)} %copy-done.11), channel_id=1, source_target_pairs={{0,64},{64,0},{1,65},{65,1},{2,66},{66,2},{3,67},{67,3},{4,68},{68... | collective-permute-start | bytes 589832 | tf_op jit(solution)/shard_map/ppermute | solution.py:57
  30.6 7.7 %collective-permute-start.2 = (bf16[128,768]{1,0:T(8,128)(2,1)S(1)}, bf16[128,768]{1,0:T(8,128)(2,1)S(1)}, u32[]{:S(2)}, u32[]{:S(2)}) collective-permute-start(bf16[128,768]{1,0:T(8,128)(2,1)S(1)} %copy-done.11), channel_id=1, source_target_pairs={{0,65},{1,64},{64,1},{65,0},{2,67},{3,66},{66,3},{67,2},{4,69},{5,... | collective-permute-start | bytes 589832 | tf_op jit(solution)/shard_map/ppermute | solution.py:58
  38.8 32.2 %copy-start.38 = (f32[512]{0:T(512)}, f32[512]{0:T(512)S(1)}, u32[]{:S(2)}) copy-start(f32[512]{0:T(512)S(1)} %add_rsqrt_fusion) | copy-start | bytes 6148
  72.8 19.7 %copy-start.2 = (bf16[512,192]{1,0:T(8,128)(2,1)S(1)}, bf16[512,192]{1,0:T(8,128)(2,1)}, u32[]{:S(2)}) copy-start(bf16[512,192]{1,0:T(8,128)(2,1)} %slice_multiply_fusion.q_ref) | copy-start | bytes 589828
  72.8 256.3 %all-gather.11.cloned.1.call-start = ((), (), s32[]{:S(2)}) async-start(), calls=%async_computation.6 | async-start | bytes 8650752 | tf_op jit(solution)/shard_map/all_gather | solution.py:826
  72.8 6.3 %collective-permute-start.4 = (bf16[128,768]{1,0:T(8,128)(2,1)S(1)}, bf16[128,768]{1,0:T(8,128)(2,1)S(1)}, u32[]{:S(2)}, u32[]{:S(2)}) collective-permute-start(bf16[128,768]{1,0:T(8,128)(2,1)S(1)} %copy-done.24), channel_id=1, source_target_pairs={{0,1},{1,0},{2,3},{3,2},{4,5},{5,4},{6,7},{7,6},{8,9},{9,8},{10,11... | collective-permute-start | bytes 589832 | tf_op jit(solution)/shard_map/ppermute | solution.py:56
  74.1 11.5 %collective-permute-start.5 = (bf16[128,768]{1,0:T(8,128)(2,1)S(1)}, bf16[128,768]{1,0:T(8,128)(2,1)S(1)}, u32[]{:S(2)}, u32[]{:S(2)}) collective-permute-start(bf16[128,768]{1,0:T(8,128)(2,1)S(1)} %copy-done.24), channel_id=1, source_target_pairs={{0,64},{64,0},{1,65},{65,1},{2,66},{66,2},{3,67},{67,3},{4,68},{68... | collective-permute-start | bytes 589832 | tf_op jit(solution)/shard_map/ppermute | solution.py:57
  76.5 12.0 %collective-permute-start.6 = (bf16[128,768]{1,0:T(8,128)(2,1)S(1)}, bf16[128,768]{1,0:T(8,128)(2,1)}, u32[]{:S(2)}, u32[]{:S(2)}) collective-permute-start(bf16[128,768]{1,0:T(8,128)(2,1)S(1)} %copy-done.24), channel_id=1, source_target_pairs={{0,65},{1,64},{64,1},{65,0},{2,67},{3,66},{66,3},{67,2},{4,69},{5,... | collective-permute-start | bytes 589832 | tf_op jit(solution)/shard_map/ppermute | solution.py:58
  89.7 69.1 %copy-start.17 = (bf16[128,768]{1,0:T(8,128)(2,1)}, bf16[128,768]{1,0:T(8,128)(2,1)S(1)}, u32[]{:S(2)}) copy-start(bf16[128,768]{1,0:T(8,128)(2,1)S(1)} %get-tuple-element.70) | copy-start | bytes 589828
  246.1 8.7 %collective-permute-start.8 = (bf16[256,192]{1,0:T(8,128)(2,1)S(1)}, bf16[256,192]{1,0:T(8,128)(2,1)S(1)}, u32[]{:S(2)}, u32[]{:S(2)}) collective-permute-start(bf16[256,192]{1,0:T(8,128)(2,1)S(1)} %get-tuple-element.96), channel_id=1, source_target_pairs={{0,62},{2,60},{4,58},{6,56},{8,54},{10,52},{12,50},{14,48},{16,46}... | collective-permute-start | bytes 294920 | tf_op jit(solution)/shard_map/ppermute | solution.py:214
  262.1 8.2 %copy-start.40 = (pred[768]{0:T(1024)(128)(4,1)S(1)}, pred[768]{0:T(1024)(128)(4,1)}, u32[]{:S(2)}) copy-start(pred[768]{0:T(1024)(128)(4,1)} %copy-done.39) | copy-start | bytes 2308
  262.1 8.2 %copy-start.42 = (pred[768]{0:T(1024)(128)(4,1)S(1)}, pred[768]{0:T(1024)(128)(4,1)}, u32[]{:S(2)}) copy-start(pred[768]{0:T(1024)(128)(4,1)} %copy-done.41) | copy-start | bytes 2308
  264.1 57.5 %all-to-all-start = ((f32[32,8,512]{2,1,0:T(8,128)}), f32[32,8,512]{2,1,0:T(8,128)S(1)}, u32[]{:S(2)}, u32[]{:S(2)}) async-start(f32[32,8,512]{2,1,0:T(8,128)} %broadcast_in_dim.42), calls=%async_computation | async-start | bytes 1048576 | tf_op jit(solution)/shard_map/all_to_all | solution.py:832
  282.8 30.5 %copy-start.9 = (bf16[512,768]{1,0:T(8,128)(2,1)S(1)}, bf16[512,768]{1,0:T(8,128)(2,1)}, u32[]{:S(2)}) copy-start(bf16[512,768]{1,0:T(8,128)(2,1)} %copy-done.8) | copy-start | bytes 2359300
  282.8 30.6 %copy-start.14 = (bf16[128,768]{1,0:T(8,128)(2,1)S(1)}, bf16[128,768]{1,0:T(8,128)(2,1)}, u32[]{:S(2)}) copy-start(bf16[128,768]{1,0:T(8,128)(2,1)} %copy-done.13) | copy-start | bytes 589828
  282.8 30.6 %copy-start.16 = (bf16[128,768]{1,0:T(8,128)(2,1)S(1)}, bf16[128,768]{1,0:T(8,128)(2,1)}, u32[]{:S(2)}) copy-start(bf16[128,768]{1,0:T(8,128)(2,1)} %copy-done.15) | copy-start | bytes 589828
  282.8 30.6 %copy-start.18 = (bf16[128,768]{1,0:T(8,128)(2,1)S(1)}, bf16[128,768]{1,0:T(8,128)(2,1)}, u32[]{:S(2)}) copy-start(bf16[128,768]{1,0:T(8,128)(2,1)} %copy-done.17) | copy-start | bytes 589828
  282.8 30.6 %copy-start.20 = (bf16[128,768]{1,0:T(8,128)(2,1)S(1)}, bf16[128,768]{1,0:T(8,128)(2,1)}, u32[]{:S(2)}) copy-start(bf16[128,768]{1,0:T(8,128)(2,1)} %copy-done.19) | copy-start | bytes 589828
  321.6 66.1 %copy-start.22 = (bf16[256,192]{1,0:T(8,128)(2,1)}, bf16[256,192]{1,0:T(8,128)(2,1)S(1)}, u32[]{:S(2)}) copy-start(bf16[256,192]{1,0:T(8,128)(2,1)S(1)} %get-tuple-element.88) | copy-start | bytes 294916
  321.6 80.0 %all-to-all-start.2 = ((bf16[32,24,1728]{2,1,0:T(8,128)(2,1)}), bf16[32,24,1728]{2,1,0:T(8,128)(2,1)}, u32[]{:S(2)}, u32[]{:S(2)}) async-start(bf16[32,24,1728]{2,1,0:T(8,128)(2,1)} %concatenate.177), calls=%async_computation.2 | async-start | bytes 5505024 | tf_op jit(solution)/shard_map/all_to_all | solution.py:884
  366.1 14.6 %collective-permute-start.10 = (bf16[256,384]{1,0:T(8,128)(2,1)S(1)}, bf16[256,384]{1,0:T(8,128)(2,1)S(1)}, u32[]{:S(2)}, u32[]{:S(2)}) collective-permute-start(bf16[256,384]{1,0:T(8,128)(2,1)S(1)} %get-tuple-element.77), channel_id=1, source_target_pairs={{0,62},{2,60},{4,58},{6,56},{8,54},{10,52},{12,50},{14,48},{16,46}... | collective-permute-start | bytes 589832 | tf_op jit(solution)/shard_map/ppermute | solution.py:214
  371.6 9.1 %collective-permute-start.9 = (bf16[256,192]{1,0:T(8,128)(2,1)}, bf16[256,192]{1,0:T(8,128)(2,1)S(1)}, u32[]{:S(2)}, u32[]{:S(2)}) collective-permute-start(bf16[256,192]{1,0:T(8,128)(2,1)} %get-tuple-element.89), channel_id=1, source_target_pairs={{0,62},{2,60},{4,58},{6,56},{8,54},{10,52},{12,50},{14,48},{16,46}... | collective-permute-start | bytes 294920 | tf_op jit(solution)/shard_map/ppermute | solution.py:214
  380.7 7.2 %copy-start.29 = (f32[768]{0:T(1024)S(1)}, f32[768]{0:T(1024)}, u32[]{:S(2)}) copy-start(f32[768]{0:T(1024)} %copy-done.28) | copy-start | bytes 9220
  380.7 7.2 %copy-start.31 = (s32[768]{0:T(1024)S(1)}, s32[768]{0:T(1024)}, u32[]{:S(2)}) copy-start(s32[768]{0:T(1024)} %copy-done.30) | copy-start | bytes 9220
  380.7 7.2 %copy-start.33 = (s32[768]{0:T(1024)S(1)}, s32[768]{0:T(1024)}, u32[]{:S(2)}) copy-start(s32[768]{0:T(1024)} %copy-done.32) | copy-start | bytes 9220
  383.8 8.1 %collective-permute-start.11 = (bf16[128,768]{1,0:T(8,128)(2,1)}, bf16[128,768]{1,0:T(8,128)(2,1)S(1)}, u32[]{:S(2)}, u32[]{:S(2)}) collective-permute-start(bf16[128,768]{1,0:T(8,128)(2,1)} %get-tuple-element.61), channel_id=1, source_target_pairs={{0,1},{1,0},{2,3},{3,2},{4,5},{5,4},{6,7},{7,6},{8,9},{9,8},{10,11... | collective-permute-start | bytes 589832 | tf_op jit(solution)/shard_map/ppermute | solution.py:56
  383.8 11.8 %collective-permute-start.12 = (bf16[128,768]{1,0:T(8,128)(2,1)}, bf16[128,768]{1,0:T(8,128)(2,1)}, u32[]{:S(2)}, u32[]{:S(2)}) collective-permute-start(bf16[128,768]{1,0:T(8,128)(2,1)} %get-tuple-element.63), channel_id=1, source_target_pairs={{0,64},{64,0},{1,65},{65,1},{2,66},{66,2},{3,67},{67,3},{4,68},{68... | collective-permute-start | bytes 589832 | tf_op jit(solution)/shard_map/ppermute | solution.py:57
  386.2 11.6 %collective-permute-start.13 = (bf16[128,768]{1,0:T(8,128)(2,1)}, bf16[128,768]{1,0:T(8,128)(2,1)}, u32[]{:S(2)}, u32[]{:S(2)}) collective-permute-start(bf16[128,768]{1,0:T(8,128)(2,1)} %get-tuple-element.62), channel_id=1, source_target_pairs={{0,65},{1,64},{64,1},{65,0},{2,67},{3,66},{66,3},{67,2},{4,69},{5,... | collective-permute-start | bytes 589832 | tf_op jit(solution)/shard_map/ppermute | solution.py:58
  387.9 9.8 %copy-start.12 = (bf16[128,768]{1,0:T(8,128)(2,1)S(1)}, bf16[128,768]{1,0:T(8,128)(2,1)}, u32[]{:S(2)}) copy-start(bf16[128,768]{1,0:T(8,128)(2,1)} %param.14) | copy-start | bytes 589828
  391.0 8.2 %copy-start.27 = (f32[128]{0:T(128)S(1)}, f32[128]{0:T(128)}, u32[]{:S(2)}) copy-start(f32[128]{0:T(128)} %broadcast_multiply_fusion.1) | copy-start | bytes 1540
  401.6 22.9 %all-to-all-start.1 = ((bf16[32,24,640]{2,1,0:T(8,128)(2,1)}), bf16[32,24,640]{2,1,0:T(8,128)(2,1)S(1)}, u32[]{:S(2)}, u32[]{:S(2)}) async-start(bf16[32,24,640]{2,1,0:T(8,128)(2,1)} %pad_maximum_fusion), calls=%async_computation.1 | async-start | bytes 1966080 | tf_op jit(solution)/shard_map/all_to_all | solution.py:884
  408.3 20.3 %copy-start.6 = (f32[128,768]{1,0:T(8,128)S(1)}, f32[128,768]{1,0:T(8,128)}, u32[]{:S(2)}) copy-start(f32[128,768]{1,0:T(8,128)} %copy-done.5) | copy-start | bytes 1179652
  424.6 4.9 %collective-permute-start.14 = (bf16[24,2368]{1,0:T(8,128)(2,1)S(1)}, bf16[24,2368]{1,0:T(8,128)(2,1)S(1)}, u32[]{:S(2)}, u32[]{:S(2)}) collective-permute-start(bf16[24,2368]{1,0:T(8,128)(2,1)S(1)} %pad_maximum_fusion.10), channel_id=1, source_target_pairs={{0,1},{1,0},{2,3},{3,2},{4,5},{5,4},{6,7},{7,6},{8,9},{9,8},{10,11... | collective-permute-start | bytes 341000 | tf_op jit(solution)/shard_map/ppermute | solution.py:56
  424.7 8.3 %collective-permute-start.15 = (bf16[24,2368]{1,0:T(8,128)(2,1)S(1)}, bf16[24,2368]{1,0:T(8,128)(2,1)S(1)}, u32[]{:S(2)}, u32[]{:S(2)}) collective-permute-start(bf16[24,2368]{1,0:T(8,128)(2,1)S(1)} %pad_maximum_fusion.10), channel_id=1, source_target_pairs={{0,64},{64,0},{1,65},{65,1},{2,66},{66,2},{3,67},{67,3},{4,68},{68... | collective-permute-start | bytes 341000 | tf_op jit(solution)/shard_map/ppermute | solution.py:57
  427.3 8.3 %collective-permute-start.16 = (bf16[24,2368]{1,0:T(8,128)(2,1)S(1)}, bf16[24,2368]{1,0:T(8,128)(2,1)S(1)}, u32[]{:S(2)}, u32[]{:S(2)}) collective-permute-start(bf16[24,2368]{1,0:T(8,128)(2,1)S(1)} %pad_maximum_fusion.10), channel_id=1, source_target_pairs={{0,65},{1,64},{64,1},{65,0},{2,67},{3,66},{66,3},{67,2},{4,69},{5,... | collective-permute-start | bytes 341000 | tf_op jit(solution)/shard_map/ppermute | solution.py:58
  (21 other events, 68.9 us)
Sparse Core Ops, SparseCore 0:
  19.4 47.2 all-gather.4
  69.7 49.1 all-gather.6
  121.2 52.7 all-gather.8
  244.8 52.6 all-gather.10
